TPU v7x, 256 devices: a whole 4x4x8 slice. The times are simulated.
256 devices in a mesh: pop: 8 (over x, core), mp: 32 (over z, y).
Axes of the slice: x: 4, y: 4, z: 8, core: 2. Of those that a mesh axis runs over, the one named last changes fastest.
Arguments:
- inputs: bfloat16 [8192, 4096], P('pop', 'mp'), may hold values from -6 to 6
- mix_gain: float32 [4096], P('mp'), may hold values from 0 to 1
- key_weight: bfloat16 [4096, 16384], P(None, 'mp'), may hold values from -0.09375 to 0.09375
- value_weight: bfloat16 [16384, 4096], P('mp'), may hold values from -0.046875 to 0.046875
- key_left: bfloat16 [2048, 4096], P('pop'), may hold values from -6 to 6
- key_right: bfloat16 [2048, 16384], P('pop', 'mp'), may hold values from -6 to 6
- value_left: bfloat16 [2048, 16384], P('pop', 'mp'), may hold values from -6 to 6
- value_right: bfloat16 [2048, 4096], P('pop'), may hold values from -6 to 6
- fitness: float32 [2048], P('pop'), may hold values from -9 to 9
Outputs:
- outputs: bfloat16 [8192, 4096], P('pop', 'mp')
- key_update: float32 [4096, 16384], P('pop', 'mp')
- value_update: float32 [16384, 4096], P('mp', 'pop')
All inputs are finite; a program needn't handle non-finite values.
Results may differ from a plain program's by a relative error of at most 0.04.
Values may be sent and summed in bfloat16 or wider, within the bound.
No kernel may reach another device: no remote copies, remote signals or barrier semaphores. Data moves between devices by JAX's collectives and lax.ppermute only.
A program may use at most 128 MiB of HBM per device.

v0:
```python
import functools
import math

import jax
import jax.numpy as jnp
from jax import lax
from jax.experimental import pallas as pl
from jax.experimental.pallas import tpu as pltpu
from jax.sharding import PartitionSpec as P

TOKS = 4
NZ = 8
NY = 4
CUT = 10
ALONG_Z = [[z * NY + y for z in range(NZ)] for y in range(NY)]
ALONG_Y = [[z * NY + y for y in range(NY)] for z in range(NZ)]
OFFSETS = (4, 3, -3, 2, -2, 1, -1, 0)
F32 = jnp.float32
BF16 = jnp.bfloat16


def along_z(x, step):
    perm = [(z * NY + y, (z + step) % NZ * NY + y) for z in range(NZ) for y in range(NY)]
    return lax.ppermute(x, "mp", perm)


def along_y(x, step):
    perm = [(z * NY + y, z * NY + (y + step) % NY) for z in range(NZ) for y in range(NY)]
    return lax.ppermute(x, "mp", perm)


def after(x, *earlier):
    return lax.optimization_barrier((x, *earlier))[0]


def ring_scatter(far, own, count, move):
    half = far[0].shape[0]
    up, down = yield move(far[0], 1), move(far[1], -1)
    for step in range(count // 2 - 1, 0, -1):
        ahead, behind = own(step).astype(F32), own(-step).astype(F32)
        if step < count // 2 - 1:
            ahead, behind = ahead + up.astype(F32), behind + down.astype(F32)
        else:
            ahead = jnp.concatenate([ahead[:half] + up.astype(F32), ahead[half:]], axis=0)
            behind = jnp.concatenate([behind[:half], behind[half:] + down.astype(F32)], axis=0)
        up, down = yield move(ahead.astype(BF16), 1), move(behind.astype(BF16), -1)
    yield own(0).astype(F32) + up.astype(F32) + down.astype(F32)


def gather_z(x):
    got = {0: x}
    up = down = x
    for step in range(1, NZ // 2):
        up, down = yield along_z(up, 1), along_z(down, -1)
        got[-step], got[step] = up, down
    got[NZ // 2] = along_z(up, 1)
    yield got


def order_kernel(me_ref, *refs):
    *blocks, out = refs
    width = blocks[0].shape[1]
    for k, block in enumerate(blocks):
        place = lax.rem(me_ref[0] + k, NY) * width
        out[:, pl.ds(pl.multiple_of(place, width), width)] = block[...]


def in_order(blocks, me):
    rows, width = blocks[0].shape
    return pl.pallas_call(
        order_kernel,
        in_specs=[pl.BlockSpec(memory_space=pltpu.SMEM)]
        + [pl.BlockSpec(memory_space=pltpu.VMEM)] * NY,
        out_specs=pl.BlockSpec(memory_space=pltpu.VMEM),
        out_shape=jax.ShapeDtypeStruct((rows, NY * width), BF16),
        cost_estimate=pl.CostEstimate(
            flops=0, bytes_accessed=4 * NY * rows * width, transcendentals=0
        ),
        name="in_order",
    )(me.reshape(1).astype(jnp.int32), *blocks)


def scatter_straight(own, offsets, move):
    return [move(own(k).astype(BF16), k) for k in offsets]


def total(own, sent):
    return sum((x.astype(F32) for x in sent), own)


def dot(a, b):
    return jnp.dot(a, b, preferred_element_type=F32)


def total_over_pop(x):
    for bit in (1, 2, 4):
        x = x + lax.ppermute(x, "pop", [(i, i ^ bit) for i in range(8)])
    return x


def columns(ref, first, step, count, width):
    parts = [
        ref[:, pl.ds(pl.multiple_of((first + step * n) * width, width), width)]
        for n in range(count)
    ]
    return jnp.concatenate(parts, axis=1)


def sums_kernel(members, carried, order_ref, *refs):
    *blocks, weight, left, base_ref, products_ref = refs
    base = products = 0.0
    if carried:
        *blocks, base_in, products_in = blocks
        base, products = base_in[...], products_in[...]
    lanes = products_ref.shape[1]
    for n, block in enumerate(blocks):
        if len(block.shape) == 2:
            tokens = block[...]
        else:
            tokens = jnp.concatenate(
                [block[y, z] for z in range(NZ) for y in range(NY)], axis=1
            )
        deep = tokens.shape[1]
        place = pl.ds(0, deep)
        if len(blocks) > 1:
            place = pl.ds(pl.multiple_of(order_ref[n] * deep, deep), deep)
        base = base + dot(tokens, weight[place, :])
        terms = tokens.astype(F32) * left[members, place].astype(F32)
        products = products + sum(terms[:, at : at + lanes] for at in range(0, deep, lanes))
    base_ref[...] = base
    products_ref[...] = products


def hidden_kernel(scale, members, carried, order_ref, *refs):
    *given, right, value_left, keyed_ref, value_dots_ref, base, products = refs
    sums_kernel(members, carried, order_ref, *given, base, products)
    left_dots = jnp.sum(products[...], axis=1, keepdims=True)
    hidden = base[...] + left_dots * (right[members, :].astype(F32) * scale)
    hidden = jnp.maximum(hidden, 0.0)
    keyed = (hidden * hidden).astype(BF16)
    keyed_ref[...] = keyed
    sums = jnp.sum(keyed.astype(F32) * value_left[members, :].astype(F32), axis=1, keepdims=True)
    value_dots_ref[...] = jnp.broadcast_to(sums, value_dots_ref.shape)


def hidden(blocks, order, members, weights, carried=(), last=True):
    key_weight, key_left, key_right, value_left = weights
    count = members.stop - members.start
    units = key_weight.shape[1]
    rows, deep = count * TOKS, blocks[0].shape[-1]
    whole = lambda x: pl.BlockSpec(x.shape, lambda i, order: (0, 0))
    part = lambda wide: pl.BlockSpec((count, wide), lambda i, order: (i, 0))
    if len(blocks[0].shape) == 2:
        specs = [part(deep) for _ in blocks]
    else:
        specs = [pl.BlockSpec((NY, NZ, count, deep), lambda i, order: (0, 0, i, 0))]
        deep = deep * NY * NZ
    specs += [part(x.shape[1]) for x in carried]
    if len(blocks) > 1:
        specs += [whole(key_weight), whole(key_left)]
    else:
        specs += [
            pl.BlockSpec((deep, units), lambda i, order: (order[0], 0)),
            pl.BlockSpec((key_left.shape[0], deep), lambda i, order: (0, order[0])),
        ]
    given = [*blocks, *carried, key_weight, key_left]
    if last:
        kernel = functools.partial(
            hidden_kernel, 1.0 / math.sqrt(key_left.shape[1]), members, bool(carried)
        )
        given, specs = given + [key_right, value_left], specs + [whole(key_right), whole(value_left)]
        scratch = [pltpu.VMEM((count, units), F32), pltpu.VMEM((count, 128), F32)]
    else:
        kernel = functools.partial(sums_kernel, members, bool(carried))
        scratch = []
    features = deep * len(blocks)
    return pl.pallas_call(
        kernel,
        grid_spec=pltpu.PrefetchScalarGridSpec(
            num_scalar_prefetch=1,
            grid=(TOKS,),
            in_specs=specs,
            out_specs=[part(units), part(128)],
            scratch_shapes=scratch,
        ),
        out_shape=[
            jax.ShapeDtypeStruct((rows, units), BF16 if last else F32),
            jax.ShapeDtypeStruct((rows, 128), F32),
        ],
        compiler_params=pltpu.CompilerParams(vmem_limit_bytes=48 * 2**20),
        cost_estimate=pl.CostEstimate(
            flops=2 * rows * features * units,
            bytes_accessed=2 * features * (rows + units + key_left.shape[0]) + 4 * rows * units,
            transcendentals=0,
        ),
        name="hidden",
    )(order, *given)


def partial_terms(keyed, value_dots, weight, rights, scale):
    terms = dot(keyed[...], weight)
    rights = rights.astype(F32) * scale
    count = rights.shape[0]
    parts = []
    for token in range(TOKS):
        rows = slice(token * count, (token + 1) * count)
        parts.append((terms[rows] + value_dots[rows, :1] * rights).astype(BF16))
    return parts


def partial_z_kernel(scale, members, order_ref, keyed, value_dots, weight, right, *outs):
    count = members.stop - members.start
    parts = partial_terms(keyed, value_dots, weight[...], right[members, :], scale)
    for token, part in enumerate(parts):
        out = outs[token * len(outs) // TOKS]
        at = token % (TOKS // len(outs)) * count
        out[0, at : at + count, :] = part


def partial_y_kernel(scale, members, order_ref, keyed, value_dots, weight, right, out):
    y = order_ref[pl.program_id(0)]
    count = members.stop - members.start
    feats = out.shape[2] // NZ
    picks = [
        pl.ds(pl.multiple_of((z * NY + y) * feats, feats), feats) for z in range(NZ)
    ]
    weights = jnp.concatenate([weight[:, pick] for pick in picks], axis=1)
    rights = jnp.concatenate([right[members, pick] for pick in picks], axis=1)
    parts = partial_terms(keyed, value_dots, weights, rights, scale)
    for token, part in enumerate(parts):
        out[0, token * count : (token + 1) * count, :] = part


def partial(keyed, value_dots, order, members, weight, right, scale, by_y=False, parts=1):
    rows, units = keyed.shape
    width = weight.shape[1]
    whole = lambda x: pl.BlockSpec(x.shape, lambda i, order: (0, 0))
    ring = NY if by_y else NZ
    if by_y:
        kernel = partial_y_kernel
        weight_specs = [whole(weight), whole(right)]
    else:
        kernel = partial_z_kernel
        weight_specs = [
            pl.BlockSpec((x.shape[0], width // NZ), lambda i, order: (0, order[i]))
            for x in (weight, right)
        ]
    shape = (len(order), rows // parts, width // ring)
    return pl.pallas_call(
        functools.partial(kernel, scale, members),
        grid_spec=pltpu.PrefetchScalarGridSpec(
            num_scalar_prefetch=1,
            grid=(len(order),),
            in_specs=[whole(keyed), whole(value_dots)] + weight_specs,
            out_specs=[pl.BlockSpec((1,) + shape[1:], lambda i, order: (i, 0, 0))] * parts,
        ),
        out_shape=[jax.ShapeDtypeStruct(shape, BF16)] * parts,
        compiler_params=pltpu.CompilerParams(vmem_limit_bytes=48 * 2**20),
        cost_estimate=pl.CostEstimate(
            flops=2 * rows * units * len(order) * (width // ring),
            bytes_accessed=2 * len(order) * (width // ring) * (rows + units),
            transcendentals=0,
        ),
        name="partial",
    )(order, keyed, value_dots, weight, right)


def shards(
    inputs,
    mix_gain,
    key_weight,
    value_weight,
    key_left,
    key_right,
    value_left,
    value_right,
    fitness,
):
    members, width = key_left.shape
    feats = inputs.shape[1]
    hidden_units = key_weight.shape[1]
    all_members = members * lax.axis_size("pop")
    all_hidden = hidden_units * lax.axis_size("mp")
    member_scale = math.sqrt(all_members)
    me = lax.axis_index("mp")
    my_z, my_y = me // NY, me % NY
    tokens = inputs.reshape(members, TOKS, feats).transpose(1, 0, 2).astype(F32)
    previous = jnp.concatenate([jnp.zeros_like(tokens[:1]), tokens[:-1]], axis=0)
    shifted = (tokens + mix_gain * (previous - tokens)).astype(BF16)
    barrier = lax.optimization_barrier
    cut = members * CUT // 16
    first, second = slice(0, cut), slice(cut, members)
    latter = shifted[:, members // 2 :].reshape(-1, feats)
    second_z = lax.all_gather(latter, "mp", axis_index_groups=ALONG_Z)
    mine = shifted[:, first].reshape(-1, feats)
    first_block = in_order([mine] + [along_y(mine, -k) for k in (1, 2, 3)], my_y)
    steps = gather_z(first_block)
    step = next(steps)

    pair = after(fitness, first_block).reshape(1, members)
    pair = jnp.concatenate([pair, pair * pair], axis=0)
    sums = total_over_pop(jnp.sum(pair, axis=1, keepdims=True)) / all_members
    mean, square = sums[:1], sums[1:]
    scores = (fitness.reshape(1, members) - mean) / jnp.sqrt(square - mean * mean + 1e-05)
    scores = scores.reshape(members)

    step, scores = barrier((step, scores))
    step = steps.send(step)

    scaled_right = (scores[:, None] * key_right.astype(F32)).astype(BF16)
    scaled_value = (scores[:, None] * value_right.astype(F32)).astype(BF16)
    member_dims = (((0,), (0,)), ((), ()))
    key_terms = lax.dot_general(
        key_left, scaled_right, member_dims, preferred_element_type=F32
    )
    value_terms = lax.dot_general(
        value_left, scaled_value, member_dims, preferred_element_type=F32
    )
    key_terms = (key_terms / member_scale).astype(BF16)
    value_terms = (value_terms / member_scale).astype(BF16)

    step, key_terms, value_terms = barrier((step, key_terms, value_terms))
    second_z = after(second_z, *step).reshape(NZ, TOKS, -1, feats)[:, :, cut - members // 2 :]
    second_all = lax.all_gather(
        second_z.reshape(NZ, -1, feats), "mp", axis_index_groups=ALONG_Y
    )
    step = barrier(steps.send(step))
    first_got = steps.send(step)
    order = ((my_z + jnp.array(OFFSETS, jnp.int32)) % NZ).astype(jnp.int32)
    key_update = lax.psum_scatter(key_terms, "pop", scatter_dimension=0, tiled=True)
    value_update = lax.psum_scatter(value_terms, "pop", scatter_dimension=1, tiled=True)

    weights = (key_weight, key_left, key_right, value_left)
    carried = hidden([first_got[k] for k in OFFSETS[1:]], order[1:], first, weights, last=False)
    first_keyed, first_dots = hidden([first_got[NZ // 2]], order[:1], first, weights, carried)

    scale = 1.0 / math.sqrt(all_hidden)
    values = (value_weight, value_right, scale)
    far = partial(first_keyed, first_dots, order[:1], first, *values, parts=2)
    (first_terms,) = partial(first_keyed, first_dots, order[1:], first, *values)
    first_steps = ring_scatter(
        [x[0] for x in far], lambda k: first_terms[OFFSETS.index(k) - 1], NZ, along_z
    )
    step = next(first_steps)
    second_keyed, second_dots = hidden(
        [after(second_all, *step)], jnp.zeros(1, jnp.int32), second, weights
    )
    order = ((my_y + jnp.array((2, 1, -1, 0), jnp.int32)) % NY).astype(jnp.int32)
    (second_terms,) = partial(second_keyed, second_dots, order, second, *values, by_y=True)
    half = second_terms.shape[1] // 2
    second_steps = ring_scatter(
        (second_terms[0, :half], second_terms[0, half:]),
        lambda k: second_terms[(2, 1, -1, 0).index(k)],
        NY,
        along_y,
    )
    step_y = next(second_steps)
    step = first_steps.send(step)
    next_y = second_steps.send(step_y)
    step = first_steps.send(step)
    step, key_update, value_update, _ = barrier((step, key_update, value_update, step_y))
    step = first_steps.send(step)
    second_sum = second_steps.send(next_y)

    def columns(x, index):
        return lax.dynamic_slice_in_dim(x, index * feats, feats, axis=1)

    own_z = lambda k: columns(second_sum, (my_z + k) % NZ)
    own_y = lambda k: columns(first_sum, (my_y + k) % NY)
    second_far = scatter_straight(own_z, (4, 3, -3), along_z)
    first_sum = first_steps.send(after(step, *second_far))
    second_near = scatter_straight(own_z, (2, -2, 1, -1), along_z)
    first_out = total(own_y(0), scatter_straight(own_y, (2, 1, -1), along_y))
    second_out = total(own_z(0), second_far + second_near)
    outputs = jnp.concatenate(
        [x.reshape(TOKS, -1, feats) for x in (first_out, second_out)], axis=1
    )
    outputs = outputs.astype(BF16).transpose(1, 0, 2).reshape(members * TOKS, feats)
    return outputs, key_update.astype(F32), value_update.astype(F32)


def solution(mesh):
    placed = (
        P("pop", "mp"),
        P("mp"),
        P(None, "mp"),
        P("mp", None),
        P("pop", None),
        P("pop", "mp"),
        P("pop", "mp"),
        P("pop", None),
        P("pop"),
    )
    return jax.shard_map(
        shards,
        mesh=mesh,
        in_specs=placed,
        out_specs=(P("pop", "mp"), P("pop", "mp"), P("mp", "pop")),
        check_vma=False,
    )
```

profile of v0, /device:TPU:64, one launch (start us, length us, event | category | flops | bytes accessed | tf_op | source)
XLA Modules:
  0.0 218.6 jit_solution(7289074684566628685)
XLA Ops:
  11.0 1.7 collective-permute-start.2
  12.6 2.9 %collective-permute-start.1 = (bf16[640,128]{1,0:T(8,128)(2,1)S(1)}, bf16[640,128]{1,0:T(8,128)(2,1)S(1)}, u32[]{:S(2)}, u32[]{:S(2)}) collective-permute-start(bf16[640,128]{1,0:T(8,128)(2,1)S(1)} %bitcast.105), channel_id=1, source_target_pairs={{0,2},{1,3},{2,0},{3,1},{4,6},{5,7},{6,4},{7,5},{8,10},{9,11},{10,... | collective-permute-start | bytes 491528 | tf_op jit(solution)/shard_map/ppermute | solution.py:29
  18.3 4.7 %collective-permute-done.1.refs_2_ = bf16[640,128]{1,0:T(8,128)(2,1)S(1)} collective-permute-done((bf16[640,128]{1,0:T(8,128)(2,1)S(1)}, bf16[640,128]{1,0:T(8,128)(2,1)S(1)}, u32[]{:S(2)}, u32[]{:S(2)}) %collective-permute-start.1) | collective-permute-done | bytes 163872 | tf_op jit(solution)/shard_map/ppermute | solution.py:29
  23.7 2.2 %in_order.1.refs_6_ = bf16[640,512]{1,0:T(8,128)(2,1)} custom-call(s32[1]{0:T(128)} %bitcast.me_ref, bf16[640,128]{1,0:T(8,128)(2,1)} %bitcast.107, bf16[640,128]{1,0:T(8,128)(2,1)} %copy-done.18, bf16[640,128]{1,0:T(8,128)(2,1)} %copy-done.17, bf16[640,128]{1,0:T(8,128)(2,1)} %copy-done.16), custom_call_target="tpu_custom_call" | custom-call | bytes 1310720 | tf_op jit(solution)/shard_map/in_order/pallas_call | solution.py:70
  26.0 2.0 collective-permute-start.3
  29.3 1.5 collective-permute-start.6
  30.8 2.0 collective-permute-done.6
  32.8 3.0 %collective-permute-start.7 = (f32[2,1]{0,1:T(1,128)S(1)}, f32[2,1]{0,1:T(1,128)S(1)}, u32[]{:S(2)}, u32[]{:S(2)}) collective-permute-start(f32[2,1]{0,1:T(1,128)S(1)} %add.224), channel_id=1, source_target_pairs={{0,128},{32,160},{64,192},{96,224},{128,0},{160,32},{192,64},{224,... | collective-permute-start | bytes 32 | tf_op jit(solution)/shard_map/ppermute | solution.py:97
  35.8 2.0 collective-permute-done.7
  41.1 8.7 %collective-permute-done.4.refs_4_ = bf16[640,512]{1,0:T(8,128)(2,1)S(1)} collective-permute-done((bf16[640,512]{1,0:T(8,128)(2,1)}, bf16[640,512]{1,0:T(8,128)(2,1)S(1)}, u32[]{:S(2)}, u32[]{:S(2)}) %collective-permute-start.4) | collective-permute-done | bytes 655392 | tf_op jit(solution)/shard_map/ppermute | solution.py:24
  49.8 3.6 %collective-permute-start.8 = (bf16[640,512]{1,0:T(8,128)(2,1)}, bf16[640,512]{1,0:T(8,128)(2,1)}, u32[]{:S(2)}, u32[]{:S(2)}) collective-permute-start(bf16[640,512]{1,0:T(8,128)(2,1)} %collective-permute-done.3.refs_5_), channel_id=1, source_target_pairs={{0,4},{1,5},{2,6},{3,7},{4,8},{5,9},{6,10},{7,11},{8,12},{9,13},{1... | collective-permute-start | bytes 1966088 | tf_op jit(solution)/shard_map/ppermute | solution.py:24
  53.6 5.0 %fusion.1 = bf16[512,4096]{0,1:T(8,128)(2,1)} fusion(bf16[256,512]{1,0:T(8,128)(2,1)S(1)} %copy-done.7, bf16[256,4096]{1,0:T(8,128)(2,1)} %right.5, f32[256]{0:T(256)S(1)} %subtract_divide_fusion), kind=kOutput, calls=%fused_computation.3 | convolution fusion | flops 1081081856 | bytes 6554624 | tf_op jit(solution)/shard_map/dot_general | solution.py:316
  58.6 3.5 %fusion = bf16[4096,512]{0,1:T(8,128)(2,1)} fusion(bf16[256,4096]{1,0:T(8,128)(2,1)S(1)} %copy-done, bf16[256,512]{1,0:T(8,128)(2,1)S(1)} %copy-done.5, f32[256]{0:T(256)S(1)} %subtract_divide_fusion), kind=kOutput, calls=%fused_computation.2 | convolution fusion | flops 1078329344 | bytes 6554624 | tf_op jit(solution)/shard_map/dot_general | solution.py:313
  62.1 5.6 %collective-permute-done.8.refs_3_ = bf16[640,512]{1,0:T(8,128)(2,1)} collective-permute-done((bf16[640,512]{1,0:T(8,128)(2,1)}, bf16[640,512]{1,0:T(8,128)(2,1)}, u32[]{:S(2)}, u32[]{:S(2)}) %collective-permute-start.8) | collective-permute-done | bytes 655392 | tf_op jit(solution)/shard_map/ppermute | solution.py:24
  67.7 2.3 %collective-permute-done.9.refs_2_ = bf16[640,512]{1,0:T(8,128)(2,1)} collective-permute-done((bf16[640,512]{1,0:T(8,128)(2,1)S(1)}, bf16[640,512]{1,0:T(8,128)(2,1)}, u32[]{:S(2)}, u32[]{:S(2)}) %collective-permute-start.9) | collective-permute-done | bytes 655392 | tf_op jit(solution)/shard_map/ppermute | solution.py:24
  69.9 2.1 slice.177
  73.3 3.0 %collective-permute-start.10 = (bf16[640,512]{1,0:T(8,128)(2,1)}, bf16[640,512]{1,0:T(8,128)(2,1)}, u32[]{:S(2)}, u32[]{:S(2)}) collective-permute-start(bf16[640,512]{1,0:T(8,128)(2,1)} %collective-permute-done.8.refs_3_), channel_id=1, source_target_pairs={{0,4},{1,5},{2,6},{3,7},{4,8},{5,9},{6,10},{7,11},{8,12},{9,13},{1... | collective-permute-start | bytes 1966088 | tf_op jit(solution)/shard_map/ppermute | solution.py:24
  76.3 12.6 %collective-permute-done.10.refs_1_ = bf16[640,512]{1,0:T(8,128)(2,1)} collective-permute-done((bf16[640,512]{1,0:T(8,128)(2,1)}, bf16[640,512]{1,0:T(8,128)(2,1)}, u32[]{:S(2)}, u32[]{:S(2)}) %collective-permute-start.10) | collective-permute-done | bytes 655392 | tf_op jit(solution)/shard_map/ppermute | solution.py:24
  88.9 2.1 collective-permute-done.11.refs_0_
  91.8 2.0 collective-permute-start.12
  96.2 8.5 %hidden.3 = (f32[640,512]{1,0:T(8,128)}, f32[640,128]{1,0:T(8,128)S(1)}) custom-call(s32[7]{0:T(128)S(1)} %slice.126.order_ref, bf16[640,512]{1,0:T(8,128)(2,1)S(1)} %copy-done.11, bf16[640,512]{1,0:T(8,128)(2,1)} %collective-permute-done.10.refs_1_, bf16[640,512]{1,0:T(8,128)(2,1)} %collective-permute-done.9.refs_2_, ...), custom_call_target="tpu_custom_call" | custom-call | flops 2348810240 | bytes 11403264 | tf_op jit(solution)/shard_map/hidden/pallas_call | solution.py:177
  107.1 2.8 %hidden.4 = (bf16[640,512]{1,0:T(8,128)(2,1)S(1)}, f32[640,128]{1,0:T(8,128)S(1)}) custom-call(s32[1]{0:T(128)S(1)} %bitcast.96, bf16[640,512]{1,0:T(8,128)(2,1)S(1)} %collective-permute-done.12.refs_0_, f32[640,512]{1,0:T(8,128)S(1)} %copy-done.6, f32[640,128]{1,0:T(8,128)S(1)} %get-tuple-element.38.refs_2_, bf16[4096,512]{1,0:T(8,128)(2,1)} %refs_1_.1, ...), custom_call_target="tpu_custom_call" | custom-call | flops 335544320 | bytes 2752512 | tf_op jit(solution)/shard_map/hidden/pallas_call | solution.py:177
  109.9 1.6 partial.4
  112.1 1.7 collective-permute-start.13
  113.9 8.4 %partial.3 = bf16[7,640,512]{2,1,0:T(8,128)(2,1)} custom-call(s32[7]{0:T(128)S(1)} %slice.126.order_ref, bf16[640,512]{1,0:T(8,128)(2,1)S(1)} %get-tuple-element.39.keyed, f32[640,128]{1,0:T(8,128)S(1)} %get-tuple-element.40.value_dots, bf16[512,4096]{1,0:T(8,128)(2,1)} %weight.5, bf16[256,4096]{1,0:T(8,128)(2,1)S(1)} %copy-done.2), custom_call_target="tpu_custom_call" | custom-call | flops 2348810240 | bytes 8257536 | tf_op jit(solution)/shard_map/partial/pallas_call | solution.py:249
  125.6 3.1 %collective-permute-start.14 = (bf16[640,512]{1,0:T(8,128)(2,1)}, bf16[640,512]{1,0:T(8,128)(2,1)}, u32[]{:S(2)}, u32[]{:S(2)}) collective-permute-start(bf16[640,512]{1,0:T(8,128)(2,1)} %pad_maximum_fusion.2), channel_id=1, source_target_pairs={{0,4},{1,5},{2,6},{3,7},{4,8},{5,9},{6,10},{7,11},{8,12},{9,13},{1... | collective-permute-start | bytes 1966088 | tf_op jit(solution)/shard_map/ppermute | solution.py:24
  129.6 6.5 %hidden.5 = (bf16[384,512]{1,0:T(8,128)(2,1)S(1)}, f32[384,128]{1,0:T(8,128)S(1)}) custom-call(s32[1]{0:T(128)} %constant.128.clone.1.order_ref, bf16[4,8,384,128]{3,2,1,0:T(8,128)(2,1)} %all-gather.5.cloned.1.call-done.refs_0_, bf16[4096,512]{1,0:T(8,128)(2,1)} %refs_1_.1, bf16[256,4096]{1,0:T(8,128)(2,1)S(1)} %copy-done.1, bf16[256,512]{1,0:T(8,128)(2,1)S(1)} %copy-done.5, ...), custom_call_target="tpu_custom_call" | custom-call | flops 1610612736 | bytes 10223616 | tf_op jit(solution)/shard_map/hidden/pallas_call | solution.py:177
  136.2 5.7 %partial.5 = bf16[4,384,1024]{2,1,0:T(8,128)(2,1)S(1)} custom-call(s32[4]{0:T(128)S(1)} %and_select_fusion.order_ref, bf16[384,512]{1,0:T(8,128)(2,1)S(1)} %get-tuple-element.47.keyed, f32[384,128]{1,0:T(8,128)S(1)} %get-tuple-element.48.value_dots, bf16[512,4096]{1,0:T(8,128)(2,1)} %weight.5, bf16[256,4096]{1,0:T(8,128)(2,1)S(1)} %copy-done.3), custom_call_target="tpu_custom_call" | custom-call | flops 1610612736 | bytes 7340032 | tf_op jit(solution)/shard_map/partial/pallas_call | solution.py:249
  143.2 2.1 collective-permute-start.20
  145.3 2.1 fusion.5
  147.5 2.1 collective-permute-start.15
  149.6 1.5 collective-permute-done.19
  153.3 2.3 %collective-permute-start.24 = (bf16[384,1024]{1,0:T(8,128)(2,1)}, bf16[384,1024]{1,0:T(8,128)(2,1)}, u32[]{:S(2)}, u32[]{:S(2)}) collective-permute-start(bf16[384,1024]{1,0:T(8,128)(2,1)} %pad_maximum_fusion.1), channel_id=1, source_target_pairs={{0,3},{1,0},{2,1},{3,2},{4,7},{5,4},{6,5},{7,6},{8,11},{9,8},{10,9... | collective-permute-start | bytes 2359304 | tf_op jit(solution)/shard_map/ppermute | solution.py:29
  156.5 3.2 %collective-permute-done.18 = bf16[640,512]{1,0:T(8,128)(2,1)} collective-permute-done((bf16[640,512]{1,0:T(8,128)(2,1)S(1)}, bf16[640,512]{1,0:T(8,128)(2,1)}, u32[]{:S(2)}, u32[]{:S(2)}) %collective-permute-start.18) | collective-permute-done | bytes 655392 | tf_op jit(solution)/shard_map/ppermute | solution.py:24
  159.8 3.2 %fusion.4 = (bf16[640,512]{1,0:T(8,128)(2,1)}, bf16[640,512]{1,0:T(8,128)(2,1)}) fusion(bf16[640,512]{1,0:T(8,128)(2,1)} %collective-permute-done.18, bf16[7,640,512]{2,1,0:T(8,128)(2,1)} %partial.3, bf16[640,512]{1,0:T(8,128)(2,1)} %collective-permute-done.15), kind=kLoop, calls=%fused_computation.9 | loop fusion | flops 2621440 | bytes 3932160 | tf_op jit(solution)/shard_map/convert_element_type | solution.py:46
  163.2 2.7 %collective-permute-start.21 = (bf16[640,512]{1,0:T(8,128)(2,1)}, bf16[640,512]{1,0:T(8,128)(2,1)}, u32[]{:S(2)}, u32[]{:S(2)}) collective-permute-start(bf16[640,512]{1,0:T(8,128)(2,1)} %get-tuple-element.65), channel_id=1, source_target_pairs={{0,4},{1,5},{2,6},{3,7},{4,8},{5,9},{6,10},{7,11},{8,12},{9,13},{1... | collective-permute-start | bytes 1966088 | tf_op jit(solution)/shard_map/ppermute | solution.py:24
  165.8 2.1 collective-permute-done.24
  168.0 3.8 %collective-permute-done.23 = bf16[384,1024]{1,0:T(8,128)(2,1)} collective-permute-done((bf16[384,1024]{1,0:T(8,128)(2,1)}, bf16[384,1024]{1,0:T(8,128)(2,1)}, u32[]{:S(2)}, u32[]{:S(2)}) %collective-permute-start.23) | collective-permute-done | bytes 786464 | tf_op jit(solution)/shard_map/ppermute | solution.py:29
  171.8 1.8 fusion.3
  175.5 1.6 collective-permute-start.25
  177.2 4.5 %collective-permute-start.27 = (bf16[384,128]{1,0:T(8,128)(2,1)S(1)}, bf16[384,128]{1,0:T(8,128)(2,1)S(1)}, u32[]{:S(2)}, u32[]{:S(2)}) collective-permute-start(bf16[384,128]{1,0:T(8,128)(2,1)S(1)} %get-tuple-element.83), channel_id=1, source_target_pairs={{0,20},{1,21},{2,22},{3,23},{4,24},{5,25},{6,26},{7,27},{8,28},{9,... | collective-permute-start | bytes 294920 | tf_op jit(solution)/shard_map/ppermute | solution.py:24
  182.2 3.5 %collective-permute-done.25 = bf16[384,128]{1,0:T(8,128)(2,1)S(1)} collective-permute-done((bf16[384,128]{1,0:T(8,128)(2,1)S(1)}, bf16[384,128]{1,0:T(8,128)(2,1)S(1)}, u32[]{:S(2)}, u32[]{:S(2)}) %collective-permute-start.25) | collective-permute-done | bytes 98336 | tf_op jit(solution)/shard_map/ppermute | solution.py:24
  185.7 5.4 %collective-permute-start.34 = (bf16[384,128]{1,0:T(8,128)(2,1)}, bf16[384,128]{1,0:T(8,128)(2,1)S(1)}, u32[]{:S(2)}, u32[]{:S(2)}) collective-permute-start(bf16[384,128]{1,0:T(8,128)(2,1)} %get-tuple-element.79), channel_id=1, source_target_pairs={{0,28},{1,29},{2,30},{3,31},{4,0},{5,1},{6,2},{7,3},{8,4},{9,5},{1... | collective-permute-start | bytes 294920 | tf_op jit(solution)/shard_map/ppermute | solution.py:24
  191.1 1.5 collective-permute-done.27
  193.9 4.1 %collective-permute-start.31 = (bf16[384,128]{1,0:T(8,128)(2,1)S(1)}, bf16[384,128]{1,0:T(8,128)(2,1)S(1)}, u32[]{:S(2)}, u32[]{:S(2)}) collective-permute-start(bf16[384,128]{1,0:T(8,128)(2,1)S(1)} %get-tuple-element.82), channel_id=1, source_target_pairs={{0,8},{1,9},{2,10},{3,11},{4,12},{5,13},{6,14},{7,15},{8,16},{9,17... | collective-permute-start | bytes 294920 | tf_op jit(solution)/shard_map/ppermute | solution.py:24
  198.1 1.7 fusion.8
  200.0 2.2 %collective-permute-start.28 = (bf16[640,128]{1,0:T(8,128)(2,1)S(1)}, bf16[640,128]{1,0:T(8,128)(2,1)S(1)}, u32[]{:S(2)}, u32[]{:S(2)}) collective-permute-start(bf16[640,128]{1,0:T(8,128)(2,1)S(1)} %get-tuple-element.85), channel_id=1, source_target_pairs={{0,2},{1,3},{2,0},{3,1},{4,6},{5,7},{6,4},{7,5},{8,10},{9,11},{10,... | collective-permute-start | bytes 491528 | tf_op jit(solution)/shard_map/ppermute | solution.py:29
  208.2 1.9 collective-permute-done.29
  (132 shorter events, 36.6 us)
Async XLA Ops:
  8.0 61.9 %all-gather.3.cloned.1.call-start = ((), (), s32[]{:S(2)}) async-start(), calls=%async_computation.4 | async-start | bytes 1179648 | tf_op jit(solution)/shard_map/all_gather | solution.py:294
  10.1 17.8 %copy-start.22 = (f32[256]{0:T(256)S(1)}, f32[256]{0:T(256)}, u32[]{:S(2)}) copy-start(f32[256]{0:T(256)} %param.19) | copy-start | bytes 3076
  10.1 43.5 %copy-start.7 = (bf16[256,512]{1,0:T(8,128)(2,1)S(1)}, bf16[256,512]{1,0:T(8,128)(2,1)}, u32[]{:S(2)}) copy-start(bf16[256,512]{1,0:T(8,128)(2,1)} %refs_4_.3) | copy-start | bytes 786436
  10.9 118.7 %all-gather.5.cloned.1.call-start = ((), (), s32[]{:S(2)}) async-start(), calls=%async_computation.5 | async-start | bytes 3932160 | tf_op jit(solution)/shard_map/all_gather | solution.py:324
  11.0 12.0 %copy-start.13 = (bf16[4,160,128]{2,1,0:T(8,128)(2,1)}, bf16[4,160,128]{2,1,0:T(8,128)(2,1)S(1)}, u32[]{:S(2)}) copy-start(bf16[4,160,128]{2,1,0:T(8,128)(2,1)S(1)} %slice.167) | copy-start | bytes 491524
  11.0 7.3 %collective-permute-start.2 = (bf16[640,128]{1,0:T(8,128)(2,1)S(1)}, bf16[640,128]{1,0:T(8,128)(2,1)S(1)}, u32[]{:S(2)}, u32[]{:S(2)}) collective-permute-start(bf16[640,128]{1,0:T(8,128)(2,1)S(1)} %bitcast.104), channel_id=1, source_target_pairs={{0,1},{1,2},{2,3},{3,0},{4,5},{5,6},{6,7},{7,4},{8,9},{9,10},{10,1... | collective-permute-start | bytes 491528 | tf_op jit(solution)/shard_map/ppermute | solution.py:29
  12.6 10.3 %collective-permute-start.1 = (bf16[640,128]{1,0:T(8,128)(2,1)S(1)}, bf16[640,128]{1,0:T(8,128)(2,1)S(1)}, u32[]{:S(2)}, u32[]{:S(2)}) collective-permute-start(bf16[640,128]{1,0:T(8,128)(2,1)S(1)} %bitcast.105), channel_id=1, source_target_pairs={{0,2},{1,3},{2,0},{3,1},{4,6},{5,7},{6,4},{7,5},{8,10},{9,11},{10,... | collective-permute-start | bytes 491528 | tf_op jit(solution)/shard_map/ppermute | solution.py:29
  15.5 7.4 %collective-permute-start = (bf16[640,128]{1,0:T(8,128)(2,1)S(1)}, bf16[640,128]{1,0:T(8,128)(2,1)S(1)}, u32[]{:S(2)}, u32[]{:S(2)}) collective-permute-start(bf16[640,128]{1,0:T(8,128)(2,1)S(1)} %bitcast.106), channel_id=1, source_target_pairs={{0,3},{1,0},{2,1},{3,2},{4,7},{5,4},{6,5},{7,6},{8,11},{9,8},{10,9... | collective-permute-start | bytes 491528 | tf_op jit(solution)/shard_map/ppermute | solution.py:29
  25.9 23.9 %collective-permute-start.4 = (bf16[640,512]{1,0:T(8,128)(2,1)}, bf16[640,512]{1,0:T(8,128)(2,1)S(1)}, u32[]{:S(2)}, u32[]{:S(2)}) collective-permute-start(bf16[640,512]{1,0:T(8,128)(2,1)} %in_order.1.refs_6_), channel_id=1, source_target_pairs={{0,28},{1,29},{2,30},{3,31},{4,0},{5,1},{6,2},{7,3},{8,4},{9,5},{1... | collective-permute-start | bytes 1966088 | tf_op jit(solution)/shard_map/ppermute | solution.py:24
  26.0 23.8 %collective-permute-start.3 = (bf16[640,512]{1,0:T(8,128)(2,1)}, bf16[640,512]{1,0:T(8,128)(2,1)}, u32[]{:S(2)}, u32[]{:S(2)}) collective-permute-start(bf16[640,512]{1,0:T(8,128)(2,1)} %in_order.1.refs_6_), channel_id=1, source_target_pairs={{0,4},{1,5},{2,6},{3,7},{4,8},{5,9},{6,10},{7,11},{8,12},{9,13},{1... | collective-permute-start | bytes 1966088 | tf_op jit(solution)/shard_map/ppermute | solution.py:24
  28.1 1.2 collective-permute-start.5
  29.3 3.5 %collective-permute-start.6 = (f32[2,1]{0,1:T(1,128)S(1)}, f32[2,1]{0,1:T(1,128)S(1)}, u32[]{:S(2)}, u32[]{:S(2)}) collective-permute-start(f32[2,1]{0,1:T(1,128)S(1)} %bitcast_add_fusion), channel_id=1, source_target_pairs={{0,64},{32,96},{64,0},{96,32},{128,192},{160,224},{192,128},{224,1... | collective-permute-start | bytes 32 | tf_op jit(solution)/shard_map/ppermute | solution.py:97
  32.8 5.0 %collective-permute-start.7 = (f32[2,1]{0,1:T(1,128)S(1)}, f32[2,1]{0,1:T(1,128)S(1)}, u32[]{:S(2)}, u32[]{:S(2)}) collective-permute-start(f32[2,1]{0,1:T(1,128)S(1)} %add.224), channel_id=1, source_target_pairs={{0,128},{32,160},{64,192},{96,224},{128,0},{160,32},{192,64},{224,... | collective-permute-start | bytes 32 | tf_op jit(solution)/shard_map/ppermute | solution.py:97
  41.1 17.5 %copy-start = (bf16[256,4096]{1,0:T(8,128)(2,1)S(1)}, bf16[256,4096]{1,0:T(8,128)(2,1)}, u32[]{:S(2)}) copy-start(bf16[256,4096]{1,0:T(8,128)(2,1)} %refs_2_.1) | copy-start | bytes 6291460
  41.1 17.5 %copy-start.5 = (bf16[256,512]{1,0:T(8,128)(2,1)S(1)}, bf16[256,512]{1,0:T(8,128)(2,1)}, u32[]{:S(2)}) copy-start(bf16[256,512]{1,0:T(8,128)(2,1)} %refs_3_.3) | copy-start | bytes 786436
  49.8 17.9 %collective-permute-start.8 = (bf16[640,512]{1,0:T(8,128)(2,1)}, bf16[640,512]{1,0:T(8,128)(2,1)}, u32[]{:S(2)}, u32[]{:S(2)}) collective-permute-start(bf16[640,512]{1,0:T(8,128)(2,1)} %collective-permute-done.3.refs_5_), channel_id=1, source_target_pairs={{0,4},{1,5},{2,6},{3,7},{4,8},{5,9},{6,10},{7,11},{8,12},{9,13},{1... | collective-permute-start | bytes 1966088 | tf_op jit(solution)/shard_map/ppermute | solution.py:24
  53.4 16.6 %collective-permute-start.9 = (bf16[640,512]{1,0:T(8,128)(2,1)S(1)}, bf16[640,512]{1,0:T(8,128)(2,1)}, u32[]{:S(2)}, u32[]{:S(2)}) collective-permute-start(bf16[640,512]{1,0:T(8,128)(2,1)S(1)} %collective-permute-done.4.refs_4_), channel_id=1, source_target_pairs={{0,28},{1,29},{2,30},{3,31},{4,0},{5,1},{6,2},{7,3},{8,4},{9,5},{1... | collective-permute-start | bytes 1966088 | tf_op jit(solution)/shard_map/ppermute | solution.py:24
  72.0 87.8 %reduce-scatter.3.cloned.1.call-start = ((), (), s32[]{:S(2)}) async-start(), calls=%async_computation.2 | async-start | bytes 4718592 | tf_op jit(solution)/shard_map/reduce_scatter | solution.py:330
  72.6 21.2 %copy-start.25 = (s32[8]{0:T(128)S(1)}, s32[8]{0:T(128)}, u32[]{:S(2)}) copy-start(s32[8]{0:T(128)} %constant.134.clone) | copy-start | bytes 100
  72.6 21.3 %copy-start.24 = (s32[4]{0:T(128)S(1)}, s32[4]{0:T(128)}, u32[]{:S(2)}) copy-start(s32[4]{0:T(128)} %constant.135.clone) | copy-start | bytes 52
  72.7 21.3 %copy-start.4 = (bf16[640,512]{1,0:T(8,128)(2,1)S(1)}, bf16[640,512]{1,0:T(8,128)(2,1)}, u32[]{:S(2)}) copy-start(bf16[640,512]{1,0:T(8,128)(2,1)} %in_order.1.refs_6_) | copy-start | bytes 1966084
  72.7 87.2 %reduce-scatter.5.cloned.1.call-start = ((), (), s32[]{:S(2)}) async-start(), calls=%async_computation.3 | async-start | bytes 4718592 | tf_op jit(solution)/shard_map/reduce_scatter | solution.py:331
  73.3 15.6 %collective-permute-start.10 = (bf16[640,512]{1,0:T(8,128)(2,1)}, bf16[640,512]{1,0:T(8,128)(2,1)}, u32[]{:S(2)}, u32[]{:S(2)}) collective-permute-start(bf16[640,512]{1,0:T(8,128)(2,1)} %collective-permute-done.8.refs_3_), channel_id=1, source_target_pairs={{0,4},{1,5},{2,6},{3,7},{4,8},{5,9},{6,10},{7,11},{8,12},{9,13},{1... | collective-permute-start | bytes 1966088 | tf_op jit(solution)/shard_map/ppermute | solution.py:24
  76.3 14.7 %collective-permute-start.11 = (bf16[640,512]{1,0:T(8,128)(2,1)}, bf16[640,512]{1,0:T(8,128)(2,1)S(1)}, u32[]{:S(2)}, u32[]{:S(2)}) collective-permute-start(bf16[640,512]{1,0:T(8,128)(2,1)} %collective-permute-done.9.refs_2_), channel_id=1, source_target_pairs={{0,28},{1,29},{2,30},{3,31},{4,0},{5,1},{6,2},{7,3},{8,4},{9,5},{1... | collective-permute-start | bytes 1966088 | tf_op jit(solution)/shard_map/ppermute | solution.py:24
  91.8 13.9 %collective-permute-start.12 = (bf16[640,512]{1,0:T(8,128)(2,1)}, bf16[640,512]{1,0:T(8,128)(2,1)S(1)}, u32[]{:S(2)}, u32[]{:S(2)}) collective-permute-start(bf16[640,512]{1,0:T(8,128)(2,1)} %collective-permute-done.10.refs_1_), channel_id=1, source_target_pairs={{0,4},{1,5},{2,6},{3,7},{4,8},{5,9},{6,10},{7,11},{8,12},{9,13},{1... | collective-permute-start | bytes 1966088 | tf_op jit(solution)/shard_map/ppermute | solution.py:24
  111.5 11.9 %collective-permute-start.16 = (bf16[320,512]{1,0:T(8,128)(2,1)S(1)}, bf16[320,512]{1,0:T(8,128)(2,1)S(1)}, u32[]{:S(2)}, u32[]{:S(2)}) collective-permute-start(bf16[320,512]{1,0:T(8,128)(2,1)S(1)} %bitcast.99), channel_id=1, source_target_pairs={{0,28},{1,29},{2,30},{3,31},{4,0},{5,1},{6,2},{7,3},{8,4},{9,5},{1... | collective-permute-start | bytes 983048 | tf_op jit(solution)/shard_map/ppermute | solution.py:24
  112.1 11.3 %collective-permute-start.13 = (bf16[320,512]{1,0:T(8,128)(2,1)S(1)}, bf16[320,512]{1,0:T(8,128)(2,1)S(1)}, u32[]{:S(2)}, u32[]{:S(2)}) collective-permute-start(bf16[320,512]{1,0:T(8,128)(2,1)S(1)} %bitcast.98), channel_id=1, source_target_pairs={{0,4},{1,5},{2,6},{3,7},{4,8},{5,9},{6,10},{7,11},{8,12},{9,13},{1... | collective-permute-start | bytes 983048 | tf_op jit(solution)/shard_map/ppermute | solution.py:24
  125.6 19.7 %collective-permute-start.14 = (bf16[640,512]{1,0:T(8,128)(2,1)}, bf16[640,512]{1,0:T(8,128)(2,1)}, u32[]{:S(2)}, u32[]{:S(2)}) collective-permute-start(bf16[640,512]{1,0:T(8,128)(2,1)} %pad_maximum_fusion.2), channel_id=1, source_target_pairs={{0,4},{1,5},{2,6},{3,7},{4,8},{5,9},{6,10},{7,11},{8,12},{9,13},{1... | collective-permute-start | bytes 1966088 | tf_op jit(solution)/shard_map/ppermute | solution.py:24
  129.6 15.7 %collective-permute-start.17 = (bf16[640,512]{1,0:T(8,128)(2,1)}, bf16[640,512]{1,0:T(8,128)(2,1)}, u32[]{:S(2)}, u32[]{:S(2)}) collective-permute-start(bf16[640,512]{1,0:T(8,128)(2,1)} %pad_maximum_fusion.3), channel_id=1, source_target_pairs={{0,28},{1,29},{2,30},{3,31},{4,0},{5,1},{6,2},{7,3},{8,4},{9,5},{1... | collective-permute-start | bytes 1966088 | tf_op jit(solution)/shard_map/ppermute | solution.py:24
  142.0 9.1 %collective-permute-start.19 = (bf16[192,1024]{1,0:T(8,128)(2,1)S(1)}, bf16[192,1024]{1,0:T(8,128)(2,1)S(1)}, u32[]{:S(2)}, u32[]{:S(2)}) collective-permute-start(bf16[192,1024]{1,0:T(8,128)(2,1)S(1)} %get-tuple-element.74), channel_id=1, source_target_pairs={{0,1},{1,2},{2,3},{3,0},{4,5},{5,6},{6,7},{7,4},{8,9},{9,10},{10,1... | collective-permute-start | bytes 1179656 | tf_op jit(solution)/shard_map/ppermute | solution.py:29
  143.2 8.8 %collective-permute-start.20 = (bf16[192,1024]{1,0:T(8,128)(2,1)S(1)}, bf16[192,1024]{1,0:T(8,128)(2,1)S(1)}, u32[]{:S(2)}, u32[]{:S(2)}) collective-permute-start(bf16[192,1024]{1,0:T(8,128)(2,1)S(1)} %get-tuple-element.77), channel_id=1, source_target_pairs={{0,3},{1,0},{2,1},{3,2},{4,7},{5,4},{6,5},{7,6},{8,11},{9,8},{10,9... | collective-permute-start | bytes 1179656 | tf_op jit(solution)/shard_map/ppermute | solution.py:29
  147.4 12.3 %collective-permute-start.18 = (bf16[640,512]{1,0:T(8,128)(2,1)S(1)}, bf16[640,512]{1,0:T(8,128)(2,1)}, u32[]{:S(2)}, u32[]{:S(2)}) collective-permute-start(bf16[640,512]{1,0:T(8,128)(2,1)S(1)} %get-tuple-element.66), channel_id=1, source_target_pairs={{0,28},{1,29},{2,30},{3,31},{4,0},{5,1},{6,2},{7,3},{8,4},{9,5},{1... | collective-permute-start | bytes 1966088 | tf_op jit(solution)/shard_map/ppermute | solution.py:24
  147.5 12.3 %collective-permute-start.15 = (bf16[640,512]{1,0:T(8,128)(2,1)S(1)}, bf16[640,512]{1,0:T(8,128)(2,1)}, u32[]{:S(2)}, u32[]{:S(2)}) collective-permute-start(bf16[640,512]{1,0:T(8,128)(2,1)S(1)} %get-tuple-element.67), channel_id=1, source_target_pairs={{0,4},{1,5},{2,6},{3,7},{4,8},{5,9},{6,10},{7,11},{8,12},{9,13},{1... | collective-permute-start | bytes 1966088 | tf_op jit(solution)/shard_map/ppermute | solution.py:24
  153.3 14.7 %collective-permute-start.24 = (bf16[384,1024]{1,0:T(8,128)(2,1)}, bf16[384,1024]{1,0:T(8,128)(2,1)}, u32[]{:S(2)}, u32[]{:S(2)}) collective-permute-start(bf16[384,1024]{1,0:T(8,128)(2,1)} %pad_maximum_fusion.1), channel_id=1, source_target_pairs={{0,3},{1,0},{2,1},{3,2},{4,7},{5,4},{6,5},{7,6},{8,11},{9,8},{10,9... | collective-permute-start | bytes 2359304 | tf_op jit(solution)/shard_map/ppermute | solution.py:29
  156.5 15.2 %collective-permute-start.23 = (bf16[384,1024]{1,0:T(8,128)(2,1)}, bf16[384,1024]{1,0:T(8,128)(2,1)}, u32[]{:S(2)}, u32[]{:S(2)}) collective-permute-start(bf16[384,1024]{1,0:T(8,128)(2,1)} %pad_maximum_fusion), channel_id=1, source_target_pairs={{0,1},{1,2},{2,3},{3,0},{4,5},{5,6},{6,7},{7,4},{8,9},{9,10},{10,1... | collective-permute-start | bytes 2359304 | tf_op jit(solution)/shard_map/ppermute | solution.py:29
  163.0 30.9 %collective-permute-start.22 = (bf16[640,512]{1,0:T(8,128)(2,1)}, bf16[640,512]{1,0:T(8,128)(2,1)}, u32[]{:S(2)}, u32[]{:S(2)}) collective-permute-start(bf16[640,512]{1,0:T(8,128)(2,1)} %get-tuple-element.64), channel_id=1, source_target_pairs={{0,28},{1,29},{2,30},{3,31},{4,0},{5,1},{6,2},{7,3},{8,4},{9,5},{1... | collective-permute-start | bytes 1966088 | tf_op jit(solution)/shard_map/ppermute | solution.py:24
  163.2 34.9 %collective-permute-start.21 = (bf16[640,512]{1,0:T(8,128)(2,1)}, bf16[640,512]{1,0:T(8,128)(2,1)}, u32[]{:S(2)}, u32[]{:S(2)}) collective-permute-start(bf16[640,512]{1,0:T(8,128)(2,1)} %get-tuple-element.65), channel_id=1, source_target_pairs={{0,4},{1,5},{2,6},{3,7},{4,8},{5,9},{6,10},{7,11},{8,12},{9,13},{1... | collective-permute-start | bytes 1966088 | tf_op jit(solution)/shard_map/ppermute | solution.py:24
  175.5 10.2 %collective-permute-start.25 = (bf16[384,128]{1,0:T(8,128)(2,1)S(1)}, bf16[384,128]{1,0:T(8,128)(2,1)S(1)}, u32[]{:S(2)}, u32[]{:S(2)}) collective-permute-start(bf16[384,128]{1,0:T(8,128)(2,1)S(1)} %get-tuple-element.78), channel_id=1, source_target_pairs={{0,16},{1,17},{2,18},{3,19},{4,20},{5,21},{6,22},{7,23},{8,24},{9,... | collective-permute-start | bytes 294920 | tf_op jit(solution)/shard_map/ppermute | solution.py:24
  177.2 15.4 %collective-permute-start.27 = (bf16[384,128]{1,0:T(8,128)(2,1)S(1)}, bf16[384,128]{1,0:T(8,128)(2,1)S(1)}, u32[]{:S(2)}, u32[]{:S(2)}) collective-permute-start(bf16[384,128]{1,0:T(8,128)(2,1)S(1)} %get-tuple-element.83), channel_id=1, source_target_pairs={{0,20},{1,21},{2,22},{3,23},{4,24},{5,25},{6,26},{7,27},{8,28},{9,... | collective-permute-start | bytes 294920 | tf_op jit(solution)/shard_map/ppermute | solution.py:24
  181.7 12.2 %collective-permute-start.26 = (bf16[384,128]{1,0:T(8,128)(2,1)S(1)}, bf16[384,128]{1,0:T(8,128)(2,1)S(1)}, u32[]{:S(2)}, u32[]{:S(2)}) collective-permute-start(bf16[384,128]{1,0:T(8,128)(2,1)S(1)} %get-tuple-element.84), channel_id=1, source_target_pairs={{0,12},{1,13},{2,14},{3,15},{4,16},{5,17},{6,18},{7,19},{8,20},{9,... | collective-permute-start | bytes 294920 | tf_op jit(solution)/shard_map/ppermute | solution.py:24
  185.7 14.3 %copy-start.19 = (bf16[384,128]{1,0:T(8,128)(2,1)}, bf16[384,128]{1,0:T(8,128)(2,1)S(1)}, u32[]{:S(2)}) copy-start(bf16[384,128]{1,0:T(8,128)(2,1)S(1)} %collective-permute-done.25) | copy-start | bytes 294916
  185.7 16.5 %collective-permute-start.34 = (bf16[384,128]{1,0:T(8,128)(2,1)}, bf16[384,128]{1,0:T(8,128)(2,1)S(1)}, u32[]{:S(2)}, u32[]{:S(2)}) collective-permute-start(bf16[384,128]{1,0:T(8,128)(2,1)} %get-tuple-element.79), channel_id=1, source_target_pairs={{0,28},{1,29},{2,30},{3,31},{4,0},{5,1},{6,2},{7,3},{8,4},{9,5},{1... | collective-permute-start | bytes 294920 | tf_op jit(solution)/shard_map/ppermute | solution.py:24
  192.6 11.0 %collective-permute-start.33 = (bf16[384,128]{1,0:T(8,128)(2,1)S(1)}, bf16[384,128]{1,0:T(8,128)(2,1)S(1)}, u32[]{:S(2)}, u32[]{:S(2)}) collective-permute-start(bf16[384,128]{1,0:T(8,128)(2,1)S(1)} %get-tuple-element.80), channel_id=1, source_target_pairs={{0,4},{1,5},{2,6},{3,7},{4,8},{5,9},{6,10},{7,11},{8,12},{9,13},{1... | collective-permute-start | bytes 294920 | tf_op jit(solution)/shard_map/ppermute | solution.py:24
  193.9 10.3 %collective-permute-start.32 = (bf16[384,128]{1,0:T(8,128)(2,1)S(1)}, bf16[384,128]{1,0:T(8,128)(2,1)S(1)}, u32[]{:S(2)}, u32[]{:S(2)}) collective-permute-start(bf16[384,128]{1,0:T(8,128)(2,1)S(1)} %get-tuple-element.81), channel_id=1, source_target_pairs={{0,24},{1,25},{2,26},{3,27},{4,28},{5,29},{6,30},{7,31},{8,0},{9,1... | collective-permute-start | bytes 294920 | tf_op jit(solution)/shard_map/ppermute | solution.py:24
  193.9 10.3 %collective-permute-start.31 = (bf16[384,128]{1,0:T(8,128)(2,1)S(1)}, bf16[384,128]{1,0:T(8,128)(2,1)S(1)}, u32[]{:S(2)}, u32[]{:S(2)}) collective-permute-start(bf16[384,128]{1,0:T(8,128)(2,1)S(1)} %get-tuple-element.82), channel_id=1, source_target_pairs={{0,8},{1,9},{2,10},{3,11},{4,12},{5,13},{6,14},{7,15},{8,16},{9,17... | collective-permute-start | bytes 294920 | tf_op jit(solution)/shard_map/ppermute | solution.py:24
  200.0 7.8 %collective-permute-start.28 = (bf16[640,128]{1,0:T(8,128)(2,1)S(1)}, bf16[640,128]{1,0:T(8,128)(2,1)S(1)}, u32[]{:S(2)}, u32[]{:S(2)}) collective-permute-start(bf16[640,128]{1,0:T(8,128)(2,1)S(1)} %get-tuple-element.85), channel_id=1, source_target_pairs={{0,2},{1,3},{2,0},{3,1},{4,6},{5,7},{6,4},{7,5},{8,10},{9,11},{10,... | collective-permute-start | bytes 491528 | tf_op jit(solution)/shard_map/ppermute | solution.py:29
  202.2 6.0 %collective-permute-start.30 = (bf16[640,128]{1,0:T(8,128)(2,1)S(1)}, bf16[640,128]{1,0:T(8,128)(2,1)S(1)}, u32[]{:S(2)}, u32[]{:S(2)}) collective-permute-start(bf16[640,128]{1,0:T(8,128)(2,1)S(1)} %get-tuple-element.86), channel_id=1, source_target_pairs={{0,3},{1,0},{2,1},{3,2},{4,7},{5,4},{6,5},{7,6},{8,11},{9,8},{10,9... | collective-permute-start | bytes 491528 | tf_op jit(solution)/shard_map/ppermute | solution.py:29
  203.6 6.5 %collective-permute-start.29 = (bf16[640,128]{1,0:T(8,128)(2,1)S(1)}, bf16[640,128]{1,0:T(8,128)(2,1)S(1)}, u32[]{:S(2)}, u32[]{:S(2)}) collective-permute-start(bf16[640,128]{1,0:T(8,128)(2,1)S(1)} %get-tuple-element.87), channel_id=1, source_target_pairs={{0,1},{1,2},{2,3},{3,0},{4,5},{5,6},{6,7},{7,4},{8,9},{9,10},{10,1... | collective-permute-start | bytes 491528 | tf_op jit(solution)/shard_map/ppermute | solution.py:29
  (17 other events, 67.0 us)
Sparse Core Ops, SparseCore 0:
  11.0 41.6 all-gather.2
  72.2 42.4 all-gather.4
Sparse Core Ops, SparseCore 1:
  75.1 41.5 reduce-scatter.2
  119.0 39.1 reduce-scatter.4
where the time goes:
time: 220 us; the launch traced here: 219 us
  waiting for transfers between devices  65 us (30%)
  starting transfers between devices  58.1 us (26%)
  Pallas kernels  35.7 us (16%)
  between operations  17.9 us (8%)
  other arithmetic  17.1 us (8%)
  local copies, waits for them, and re-layouts  16.3 us (7%)
  matrix products  8.49 us (4%)
    ppermute x22, waiting for transfers between devices, along_z(): return lax.ppermute(x, 'mp', perm)  41.9 us
    ppermute x22, starting transfers between devices, along_z(): return lax.ppermute(x, 'mp', perm)  37.6 us
    pallas_call x3, Pallas kernels, hidden(): pl.pallas_call(kernel, grid_spec=pltpu.PrefetchScalarGridSpec(num_scalar_...  17.8 us
    ppermute x10, waiting for transfers between devices, along_y(): return lax.ppermute(x, 'mp', perm)  16.8 us
    ppermute x10, starting transfers between devices, along_y(): return lax.ppermute(x, 'mp', perm)  15.8 us
    pallas_call x3, Pallas kernels, partial(): pl.pallas_call(functools.partial(kernel, scale, members), grid_spec=pltpu...  15.7 us
    unnamed x54, local copies, waits for them, and re-layouts  8.74 us
    convert_element_type x2, other arithmetic, ring_scatter(): behind.astype(BF16)  5.28 us
  transfers between devices with their start and end apart: 39, of which 22 were waited for; matrix products, arithmetic and copies ran while one was open for 14% of the time, Pallas kernels for 16%

commit v1 on v0

--- a/solution.py
+++ b/solution.py
@@ -15,6 +15,7 @@
 ALONG_Z = [[z * NY + y for z in range(NZ)] for y in range(NY)]
 ALONG_Y = [[z * NY + y for y in range(NY)] for z in range(NZ)]
 OFFSETS = (4, 3, -3, 2, -2, 1, -1, 0)
+VMEM = 32 * 2**20
 F32 = jnp.float32
 BF16 = jnp.bfloat16
 
@@ -41,9 +42,10 @@
         if step < count // 2 - 1:
             ahead, behind = ahead + up.astype(F32), behind + down.astype(F32)
         else:
-            ahead = jnp.concatenate([ahead[:half] + up.astype(F32), ahead[half:]], axis=0)
-            behind = jnp.concatenate([behind[:half], behind[half:] + down.astype(F32)], axis=0)
-        up, down = yield move(ahead.astype(BF16), 1), move(behind.astype(BF16), -1)
+            ahead = ahead + jnp.pad(up.astype(F32), ((0, half), (0, 0)))
+            behind = behind + jnp.pad(down.astype(F32), ((half, 0), (0, 0)))
+        ahead, behind = lax.optimization_barrier((ahead.astype(BF16), behind.astype(BF16)))
+        up, down = yield move(ahead, 1), move(behind, -1)
     yield own(0).astype(F32) + up.astype(F32) + down.astype(F32)
 
 
@@ -187,7 +189,7 @@
             jax.ShapeDtypeStruct((rows, units), BF16 if last else F32),
             jax.ShapeDtypeStruct((rows, 128), F32),
         ],
-        compiler_params=pltpu.CompilerParams(vmem_limit_bytes=48 * 2**20),
+        compiler_params=pltpu.CompilerParams(vmem_limit_bytes=VMEM),
         cost_estimate=pl.CostEstimate(
             flops=2 * rows * features * units,
             bytes_accessed=2 * features * (rows + units + key_left.shape[0]) + 4 * rows * units,
@@ -255,7 +257,7 @@
             out_specs=[pl.BlockSpec((1,) + shape[1:], lambda i, order: (i, 0, 0))] * parts,
         ),
         out_shape=[jax.ShapeDtypeStruct(shape, BF16)] * parts,
-        compiler_params=pltpu.CompilerParams(vmem_limit_bytes=48 * 2**20),
+        compiler_params=pltpu.CompilerParams(vmem_limit_bytes=VMEM),
         cost_estimate=pl.CostEstimate(
             flops=2 * rows * units * len(order) * (width // ring),
             bytes_accessed=2 * len(order) * (width // ring) * (rows + units),
@@ -341,7 +343,7 @@
     first_steps = ring_scatter(
         [x[0] for x in far], lambda k: first_terms[OFFSETS.index(k) - 1], NZ, along_z
     )
-    step = next(first_steps)
+    step = barrier(next(first_steps))
     second_keyed, second_dots = hidden(
         [after(second_all, *step)], jnp.zeros(1, jnp.int32), second, weights
     )
@@ -356,9 +358,9 @@
     )
     step_y = next(second_steps)
     step = first_steps.send(step)
-    next_y = second_steps.send(step_y)
+    next_y = second_steps.send(after(step_y, *step))
     step = first_steps.send(step)
-    step, key_update, value_update, _ = barrier((step, key_update, value_update, step_y))
+    step, key_update, value_update = barrier((step, key_update, value_update))
     step = first_steps.send(step)
     second_sum = second_steps.send(next_y)
 
@@ -368,8 +370,8 @@
     own_z = lambda k: columns(second_sum, (my_z + k) % NZ)
     own_y = lambda k: columns(first_sum, (my_y + k) % NY)
     second_far = scatter_straight(own_z, (4, 3, -3), along_z)
-    first_sum = first_steps.send(after(step, *second_far))
     second_near = scatter_straight(own_z, (2, -2, 1, -1), along_z)
+    first_sum = first_steps.send(after(step, *second_far, *second_near))
     first_out = total(own_y(0), scatter_straight(own_y, (2, 1, -1), along_y))
     second_out = total(own_z(0), second_far + second_near)
     outputs = jnp.concatenate(

time: 220 us -> 226 us (1.027)
  waiting for transfers between devices: 65 us -> 79.3 us
  Pallas kernels: 35.7 us -> 23.9 us
  local copies, waits for them, and re-layouts: 16.3 us -> 21.5 us
    ppermute x22, waiting for transfers between devices: 41.9 us -> 57.5 us  [along_z(): return lax.ppermute(x, 'mp', perm)]
    pallas_call x3, Pallas kernels: 15.7 us -> 8.56 us  [partial(): pl.pallas_call(functools.partial(kernel, scale, members), grid_spec=pltpu...]
    unnamed x54 -> x68, local copies, waits for them, and re-layouts: 8.74 us -> 15.8 us
    pallas_call x3, Pallas kernels: 17.8 us -> 13.2 us  [hidden(): pl.pallas_call(kernel, grid_spec=pltpu.PrefetchScalarGridSpec(num_scalar_...]
    convert_element_type x2 -> x4, other arithmetic: 5.28 us -> 9.12 us  [ring_scatter(): behind.astype(BF16)]
    concatenate x4 -> x0, other arithmetic: 3.65 us -> none  [the longest x2 1.84 us: ring_scatter(): jnp.concatenate([ahead[:half] + up.astype(F32), ahead[half:]], axis=0)]
    ppermute x10, waiting for transfers between devices: 16.8 us -> 13.2 us  [along_y(): return lax.ppermute(x, 'mp', perm)]
    ppermute x22, starting transfers between devices: 37.6 us -> 35.1 us  [along_z(): return lax.ppermute(x, 'mp', perm)]
  transfers between devices with their start and end apart: 39 -> 39, of which waited for: 22 -> 26; matrix products, arithmetic and copies ran while one was open for 14% -> 11% of each run, Pallas kernels for 16% -> 11%
where the time goes in v1:
time: 226 us; the launch traced here: 224 us
  waiting for transfers between devices  79.3 us (35%)
  starting transfers between devices  57.2 us (25%)
  Pallas kernels  23.9 us (11%)
  local copies, waits for them, and re-layouts  21.5 us (10%)
  between operations  17.9 us (8%)
  other arithmetic  15.8 us (7%)
  matrix products  8.43 us (4%)
    ppermute x22, waiting for transfers between devices, along_z(): return lax.ppermute(x, 'mp', perm)  57.5 us
    ppermute x22, starting transfers between devices, along_z(): return lax.ppermute(x, 'mp', perm)  35.1 us
    ppermute x10, starting transfers between devices, along_y(): return lax.ppermute(x, 'mp', perm)  17.3 us
    unnamed x68, local copies, waits for them, and re-layouts  15.8 us
    pallas_call x3, Pallas kernels, hidden(): pl.pallas_call(kernel, grid_spec=pltpu.PrefetchScalarGridSpec(num_scalar_...  13.2 us
    ppermute x10, waiting for transfers between devices, along_y(): return lax.ppermute(x, 'mp', perm)  13.2 us
    convert_element_type x4, other arithmetic, ring_scatter(): behind.astype(BF16)  9.12 us
    pallas_call x3, Pallas kernels, partial(): pl.pallas_call(functools.partial(kernel, scale, members), grid_spec=pltpu...  8.56 us
  transfers between devices with their start and end apart: 39, of which 26 were waited for; matrix products, arithmetic and copies ran while one was open for 11% of the time, Pallas kernels for 11%

profile of v1, /device:TPU:64, one launch (start us, length us, event | category | flops | bytes accessed | tf_op | source)
XLA Modules:
  0.0 224.0 jit_solution(15870003206170120010)
XLA Ops:
  12.6 2.9 %collective-permute-start.1 = (bf16[640,128]{1,0:T(8,128)(2,1)S(1)}, bf16[640,128]{1,0:T(8,128)(2,1)S(1)}, u32[]{:S(2)}, u32[]{:S(2)}) collective-permute-start(bf16[640,128]{1,0:T(8,128)(2,1)S(1)} %bitcast.97), channel_id=1, source_target_pairs={{0,2},{1,3},{2,0},{3,1},{4,6},{5,7},{6,4},{7,5},{8,10},{9,11},{10,... | collective-permute-start | bytes 491528 | tf_op jit(solution)/shard_map/ppermute | solution.py:30
  18.3 4.7 %collective-permute-done.1.refs_2_ = bf16[640,128]{1,0:T(8,128)(2,1)S(1)} collective-permute-done((bf16[640,128]{1,0:T(8,128)(2,1)S(1)}, bf16[640,128]{1,0:T(8,128)(2,1)S(1)}, u32[]{:S(2)}, u32[]{:S(2)}) %collective-permute-start.1) | collective-permute-done | bytes 163872 | tf_op jit(solution)/shard_map/ppermute | solution.py:30
  23.7 2.2 in_order.1.refs_6_
  25.9 2.0 collective-permute-start.3
  30.7 2.0 collective-permute-done.6
  32.8 3.0 %collective-permute-start.7 = (f32[2,1]{0,1:T(1,128)S(1)}, f32[2,1]{0,1:T(1,128)S(1)}, u32[]{:S(2)}, u32[]{:S(2)}) collective-permute-start(f32[2,1]{0,1:T(1,128)S(1)} %add.232), channel_id=1, source_target_pairs={{0,128},{32,160},{64,192},{96,224},{128,0},{160,32},{192,64},{224,... | collective-permute-start | bytes 32 | tf_op jit(solution)/shard_map/ppermute | solution.py:99
  35.8 2.0 collective-permute-done.7
  41.1 8.7 %collective-permute-done.4.refs_4_ = bf16[640,512]{1,0:T(8,128)(2,1)S(1)} collective-permute-done((bf16[640,512]{1,0:T(8,128)(2,1)}, bf16[640,512]{1,0:T(8,128)(2,1)S(1)}, u32[]{:S(2)}, u32[]{:S(2)}) %collective-permute-start.4) | collective-permute-done | bytes 655392 | tf_op jit(solution)/shard_map/ppermute | solution.py:25
  49.7 3.6 %collective-permute-start.8 = (bf16[640,512]{1,0:T(8,128)(2,1)}, bf16[640,512]{1,0:T(8,128)(2,1)}, u32[]{:S(2)}, u32[]{:S(2)}) collective-permute-start(bf16[640,512]{1,0:T(8,128)(2,1)} %collective-permute-done.3.refs_5_), channel_id=1, source_target_pairs={{0,4},{1,5},{2,6},{3,7},{4,8},{5,9},{6,10},{7,11},{8,12},{9,13},{1... | collective-permute-start | bytes 1966088 | tf_op jit(solution)/shard_map/ppermute | solution.py:25
  53.6 5.0 %fusion.1 = bf16[512,4096]{0,1:T(8,128)(2,1)} fusion(bf16[256,512]{1,0:T(8,128)(2,1)S(1)} %copy-done.11, bf16[256,4096]{1,0:T(8,128)(2,1)} %right.5, f32[256]{0:T(256)S(1)} %subtract_divide_fusion), kind=kOutput, calls=%fused_computation.3 | convolution fusion | flops 1081081856 | bytes 6554624 | tf_op jit(solution)/shard_map/dot_general | solution.py:318
  58.6 3.4 %fusion = bf16[4096,512]{0,1:T(8,128)(2,1)} fusion(bf16[256,4096]{1,0:T(8,128)(2,1)S(1)} %copy-done.4, bf16[256,512]{1,0:T(8,128)(2,1)S(1)} %copy-done.10, f32[256]{0:T(256)S(1)} %subtract_divide_fusion), kind=kOutput, calls=%fused_computation.2 | convolution fusion | flops 1078329344 | bytes 6554624 | tf_op jit(solution)/shard_map/dot_general | solution.py:315
  62.0 5.7 %collective-permute-done.8.refs_3_ = bf16[640,512]{1,0:T(8,128)(2,1)} collective-permute-done((bf16[640,512]{1,0:T(8,128)(2,1)}, bf16[640,512]{1,0:T(8,128)(2,1)}, u32[]{:S(2)}, u32[]{:S(2)}) %collective-permute-start.8) | collective-permute-done | bytes 655392 | tf_op jit(solution)/shard_map/ppermute | solution.py:25
  67.7 2.3 %collective-permute-done.9.refs_2_ = bf16[640,512]{1,0:T(8,128)(2,1)} collective-permute-done((bf16[640,512]{1,0:T(8,128)(2,1)S(1)}, bf16[640,512]{1,0:T(8,128)(2,1)}, u32[]{:S(2)}, u32[]{:S(2)}) %collective-permute-start.9) | collective-permute-done | bytes 655392 | tf_op jit(solution)/shard_map/ppermute | solution.py:25
  69.9 2.1 slice.92
  73.2 3.0 %collective-permute-start.10 = (bf16[640,512]{1,0:T(8,128)(2,1)}, bf16[640,512]{1,0:T(8,128)(2,1)}, u32[]{:S(2)}, u32[]{:S(2)}) collective-permute-start(bf16[640,512]{1,0:T(8,128)(2,1)} %collective-permute-done.8.refs_3_), channel_id=1, source_target_pairs={{0,4},{1,5},{2,6},{3,7},{4,8},{5,9},{6,10},{7,11},{8,12},{9,13},{1... | collective-permute-start | bytes 1966088 | tf_op jit(solution)/shard_map/ppermute | solution.py:25
  76.3 12.6 %collective-permute-done.10.refs_1_ = bf16[640,512]{1,0:T(8,128)(2,1)} collective-permute-done((bf16[640,512]{1,0:T(8,128)(2,1)}, bf16[640,512]{1,0:T(8,128)(2,1)}, u32[]{:S(2)}, u32[]{:S(2)}) %collective-permute-start.10) | collective-permute-done | bytes 655392 | tf_op jit(solution)/shard_map/ppermute | solution.py:25
  88.9 2.1 collective-permute-done.11.refs_0_
  91.8 2.0 collective-permute-start.12
  93.9 2.3 %copy-done = bf16[4096,512]{1,0:T(8,128)(2,1)S(1)} copy-done((bf16[4096,512]{1,0:T(8,128)(2,1)S(1)}, bf16[4096,512]{1,0:T(8,128)(2,1)}, u32[]{:S(2)}) %copy-start) | copy-done | bytes 4194328
  98.4 5.3 %hidden.3 = (f32[640,512]{1,0:T(8,128)S(1)}, f32[640,128]{1,0:T(8,128)S(1)}) custom-call(s32[7]{0:T(128)S(1)} %slice.62.order_ref, bf16[640,512]{1,0:T(8,128)(2,1)S(1)} %copy-done.15, bf16[640,512]{1,0:T(8,128)(2,1)} %collective-permute-done.10.refs_1_, bf16[640,512]{1,0:T(8,128)(2,1)} %collective-permute-done.9.refs_2_, ...), custom_call_target="tpu_custom_call" | custom-call | flops 2348810240 | bytes 11403264 | tf_op jit(solution)/shard_map/hidden/pallas_call | solution.py:179
  103.8 2.0 collective-permute-done.12.refs_0_
  105.8 3.9 %hidden.4 = (bf16[640,512]{1,0:T(8,128)(2,1)S(1)}, f32[640,128]{1,0:T(8,128)S(1)}) custom-call(s32[1]{0:T(128)S(1)} %bitcast.88, bf16[640,512]{1,0:T(8,128)(2,1)} %collective-permute-done.12.refs_0_, f32[640,512]{1,0:T(8,128)S(1)} %get-tuple-element.49.refs_1_, f32[640,128]{1,0:T(8,128)S(1)} %get-tuple-element.50.refs_2_, bf16[4096,512]{1,0:T(8,128)(2,1)S(1)} %copy-done, ...), custom_call_target="tpu_custom_call" | custom-call | flops 335544320 | bytes 2752512 | tf_op jit(solution)/shard_map/hidden/pallas_call | solution.py:179
  112.6 4.6 %partial.3 = bf16[7,640,512]{2,1,0:T(8,128)(2,1)S(1)} custom-call(s32[7]{0:T(128)S(1)} %slice.62.order_ref, bf16[640,512]{1,0:T(8,128)(2,1)S(1)} %get-tuple-element.51.keyed, f32[640,128]{1,0:T(8,128)S(1)} %get-tuple-element.52.value_dots, bf16[512,4096]{1,0:T(8,128)(2,1)S(1)} %copy-done.2, bf16[256,4096]{1,0:T(8,128)(2,1)S(1)} %copy-done.5), custom_call_target="tpu_custom_call" | custom-call | flops 2348810240 | bytes 8257536 | tf_op jit(solution)/shard_map/partial/pallas_call | solution.py:251
  120.7 3.1 %collective-permute-start.15 = (bf16[640,512]{1,0:T(8,128)(2,1)}, bf16[640,512]{1,0:T(8,128)(2,1)}, u32[]{:S(2)}, u32[]{:S(2)}) collective-permute-start(bf16[640,512]{1,0:T(8,128)(2,1)} %get-tuple-element.57), channel_id=1, source_target_pairs={{0,4},{1,5},{2,6},{3,7},{4,8},{5,9},{6,10},{7,11},{8,12},{9,13},{1... | collective-permute-start | bytes 1966088 | tf_op jit(solution)/shard_map/ppermute | solution.py:25
  123.9 2.2 copy-done.1
  126.1 1.9 copy-done.8
  127.9 3.9 %hidden.5 = (bf16[384,512]{1,0:T(8,128)(2,1)S(1)}, f32[384,128]{1,0:T(8,128)S(1)}) custom-call(s32[1]{0:T(128)} %constant.131.clone.1.order_ref, bf16[4,8,384,128]{3,2,1,0:T(8,128)(2,1)S(1)} %copy-done.8, bf16[4096,512]{1,0:T(8,128)(2,1)S(1)} %copy-done.1, bf16[256,4096]{1,0:T(8,128)(2,1)S(1)} %copy-done.4, bf16[256,512]{1,0:T(8,128)(2,1)S(1)} %copy-done.10, ...), custom_call_target="tpu_custom_call" | custom-call | flops 1610612736 | bytes 10223616 | tf_op jit(solution)/shard_map/hidden/pallas_call | solution.py:179
  131.9 3.4 %partial.5 = bf16[4,384,1024]{2,1,0:T(8,128)(2,1)S(1)} custom-call(s32[4]{0:T(128)S(1)} %and_select_fusion.order_ref, bf16[384,512]{1,0:T(8,128)(2,1)S(1)} %get-tuple-element.69.keyed, f32[384,128]{1,0:T(8,128)S(1)} %get-tuple-element.70.value_dots, bf16[512,4096]{1,0:T(8,128)(2,1)S(1)} %copy-done.3, bf16[256,4096]{1,0:T(8,128)(2,1)S(1)} %copy-done.6), custom_call_target="tpu_custom_call" | custom-call | flops 1610612736 | bytes 7340032 | tf_op jit(solution)/shard_map/partial/pallas_call | solution.py:251
  135.3 3.2 %collective-permute-start.22 = (bf16[192,1024]{1,0:T(8,128)(2,1)S(1)}, bf16[192,1024]{1,0:T(8,128)(2,1)S(1)}, u32[]{:S(2)}, u32[]{:S(2)}) collective-permute-start(bf16[192,1024]{1,0:T(8,128)(2,1)S(1)} %get-tuple-element.96), channel_id=1, source_target_pairs={{0,3},{1,0},{2,1},{3,2},{4,7},{5,4},{6,5},{7,6},{8,11},{9,8},{10,9... | collective-permute-start | bytes 1179656 | tf_op jit(solution)/shard_map/ppermute | solution.py:30
  138.5 3.2 %fusion.7 = (bf16[640,512]{1,0:T(8,128)(2,1)}, bf16[640,512]{1,0:T(8,128)(2,1)}) fusion(bf16[640,512]{1,0:T(8,128)(2,1)} %collective-permute-done.16, bf16[7,640,512]{2,1,0:T(8,128)(2,1)} %copy-done.7, bf16[640,512]{1,0:T(8,128)(2,1)} %collective-permute-done.15), kind=kLoop, calls=%fused_computation.15 | loop fusion | flops 2621440 | bytes 3932160 | tf_op jit(solution)/shard_map/convert_element_type | solution.py:47
  141.7 2.0 collective-permute-start.17
  143.8 3.7 %collective-permute-done.21 = bf16[192,1024]{1,0:T(8,128)(2,1)S(1)} collective-permute-done((bf16[192,1024]{1,0:T(8,128)(2,1)S(1)}, bf16[192,1024]{1,0:T(8,128)(2,1)S(1)}, u32[]{:S(2)}, u32[]{:S(2)}) %collective-permute-start.21) | collective-permute-done | bytes 393248 | tf_op jit(solution)/shard_map/ppermute | solution.py:30
  149.0 3.2 %collective-permute-start.24 = (bf16[384,1024]{1,0:T(8,128)(2,1)}, bf16[384,1024]{1,0:T(8,128)(2,1)}, u32[]{:S(2)}, u32[]{:S(2)}) collective-permute-start(bf16[384,1024]{1,0:T(8,128)(2,1)} %get-tuple-element.74), channel_id=1, source_target_pairs={{0,3},{1,0},{2,1},{3,2},{4,7},{5,4},{6,5},{7,6},{8,11},{9,8},{10,9... | collective-permute-start | bytes 2359304 | tf_op jit(solution)/shard_map/ppermute | solution.py:30
  152.2 1.9 collective-permute-done.17
  154.1 2.0 collective-permute-done.18
  156.1 2.3 %reduce-scatter.5.cloned.1.call-done = bf16[512,512]{0,1:T(8,128)(2,1)} async-done(((bf16[512,4096]{0,1:T(8,128)(2,1)}), bf16[512,512]{0,1:T(8,128)(2,1)}) %reduce-scatter.5.cloned.1.call-update) | async-done | bytes 524304 | tf_op jit(solution)/shard_map/reduce_scatter | solution.py:333
  158.4 3.2 %fusion.6 = (bf16[640,512]{1,0:T(8,128)(2,1)}, bf16[640,512]{1,0:T(8,128)(2,1)}) fusion(bf16[640,512]{1,0:T(8,128)(2,1)} %collective-permute-done.18, bf16[7,640,512]{2,1,0:T(8,128)(2,1)} %copy-done.7, bf16[640,512]{1,0:T(8,128)(2,1)} %collective-permute-done.17), kind=kLoop, calls=%fused_computation.13 | loop fusion | flops 2621440 | bytes 3932160 | tf_op jit(solution)/shard_map/convert_element_type | solution.py:47
  161.6 2.0 collective-permute-start.19
  167.8 3.4 %collective-permute-start.25 = (bf16[384,128]{1,0:T(8,128)(2,1)S(1)}, bf16[384,128]{1,0:T(8,128)(2,1)S(1)}, u32[]{:S(2)}, u32[]{:S(2)}) collective-permute-start(bf16[384,128]{1,0:T(8,128)(2,1)S(1)} %get-tuple-element.98), channel_id=1, source_target_pairs={{0,16},{1,17},{2,18},{3,19},{4,20},{5,21},{6,22},{7,23},{8,24},{9,... | collective-permute-start | bytes 294920 | tf_op jit(solution)/shard_map/ppermute | solution.py:25
  173.2 8.9 %collective-permute-done.25 = bf16[384,128]{1,0:T(8,128)(2,1)S(1)} collective-permute-done((bf16[384,128]{1,0:T(8,128)(2,1)S(1)}, bf16[384,128]{1,0:T(8,128)(2,1)S(1)}, u32[]{:S(2)}, u32[]{:S(2)}) %collective-permute-start.25) | collective-permute-done | bytes 98336 | tf_op jit(solution)/shard_map/ppermute | solution.py:25
  182.2 2.4 %collective-permute-start.29 = (bf16[384,128]{1,0:T(8,128)(2,1)S(1)}, bf16[384,128]{1,0:T(8,128)(2,1)}, u32[]{:S(2)}, u32[]{:S(2)}) collective-permute-start(bf16[384,128]{1,0:T(8,128)(2,1)S(1)} %get-tuple-element.101), channel_id=1, source_target_pairs={{0,24},{1,25},{2,26},{3,27},{4,28},{5,29},{6,30},{7,31},{8,0},{9,1... | collective-permute-start | bytes 294920 | tf_op jit(solution)/shard_map/ppermute | solution.py:25
  184.6 4.0 %collective-permute-done.31 = bf16[384,128]{1,0:T(8,128)(2,1)} collective-permute-done((bf16[384,128]{1,0:T(8,128)(2,1)S(1)}, bf16[384,128]{1,0:T(8,128)(2,1)}, u32[]{:S(2)}, u32[]{:S(2)}) %collective-permute-start.31) | collective-permute-done | bytes 98336 | tf_op jit(solution)/shard_map/ppermute | solution.py:25
  188.6 2.8 %collective-permute-start.28 = (bf16[384,128]{1,0:T(8,128)(2,1)S(1)}, bf16[384,128]{1,0:T(8,128)(2,1)S(1)}, u32[]{:S(2)}, u32[]{:S(2)}) collective-permute-start(bf16[384,128]{1,0:T(8,128)(2,1)S(1)} %get-tuple-element.102), channel_id=1, source_target_pairs={{0,8},{1,9},{2,10},{3,11},{4,12},{5,13},{6,14},{7,15},{8,16},{9,17... | collective-permute-start | bytes 294920 | tf_op jit(solution)/shard_map/ppermute | solution.py:25
  194.0 2.4 %collective-permute-start.26 = (bf16[384,128]{1,0:T(8,128)(2,1)S(1)}, bf16[384,128]{1,0:T(8,128)(2,1)S(1)}, u32[]{:S(2)}, u32[]{:S(2)}) collective-permute-start(bf16[384,128]{1,0:T(8,128)(2,1)S(1)} %get-tuple-element.104), channel_id=1, source_target_pairs={{0,12},{1,13},{2,14},{3,15},{4,16},{5,17},{6,18},{7,19},{8,20},{9,... | collective-permute-start | bytes 294920 | tf_op jit(solution)/shard_map/ppermute | solution.py:25
  196.4 3.7 %collective-permute-done.27 = bf16[384,128]{1,0:T(8,128)(2,1)S(1)} collective-permute-done((bf16[384,128]{1,0:T(8,128)(2,1)S(1)}, bf16[384,128]{1,0:T(8,128)(2,1)S(1)}, u32[]{:S(2)}, u32[]{:S(2)}) %collective-permute-start.27) | collective-permute-done | bytes 98336 | tf_op jit(solution)/shard_map/ppermute | solution.py:25
  200.2 1.9 collective-permute-done.26
  202.8 1.8 fusion.12
  204.7 3.0 %collective-permute-start.32 = (bf16[640,128]{1,0:T(8,128)(2,1)S(1)}, bf16[640,128]{1,0:T(8,128)(2,1)S(1)}, u32[]{:S(2)}, u32[]{:S(2)}) collective-permute-start(bf16[640,128]{1,0:T(8,128)(2,1)S(1)} %get-tuple-element.105), channel_id=1, source_target_pairs={{0,2},{1,3},{2,0},{3,1},{4,6},{5,7},{6,4},{7,5},{8,10},{9,11},{10,... | collective-permute-start | bytes 491528 | tf_op jit(solution)/shard_map/ppermute | solution.py:30
  (141 shorter events, 43.1 us)
Async XLA Ops:
  8.0 61.9 %all-gather.3.cloned.1.call-start = ((), (), s32[]{:S(2)}) async-start(), calls=%async_computation.4 | async-start | bytes 1179648 | tf_op jit(solution)/shard_map/all_gather | solution.py:296
  10.1 17.8 %copy-start.29 = (f32[256]{0:T(256)S(1)}, f32[256]{0:T(256)}, u32[]{:S(2)}) copy-start(f32[256]{0:T(256)} %param.19) | copy-start | bytes 3076
  10.1 43.4 %copy-start.11 = (bf16[256,512]{1,0:T(8,128)(2,1)S(1)}, bf16[256,512]{1,0:T(8,128)(2,1)}, u32[]{:S(2)}) copy-start(bf16[256,512]{1,0:T(8,128)(2,1)} %refs_4_.3) | copy-start | bytes 786436
  10.9 113.0 %all-gather.5.cloned.1.call-start = ((), (), s32[]{:S(2)}) async-start(), calls=%async_computation.5 | async-start | bytes 3932160 | tf_op jit(solution)/shard_map/all_gather | solution.py:326
  11.0 12.0 %copy-start.17 = (bf16[4,160,128]{2,1,0:T(8,128)(2,1)}, bf16[4,160,128]{2,1,0:T(8,128)(2,1)S(1)}, u32[]{:S(2)}) copy-start(bf16[4,160,128]{2,1,0:T(8,128)(2,1)S(1)} %slice.83) | copy-start | bytes 491524
  11.0 7.3 %collective-permute-start.2 = (bf16[640,128]{1,0:T(8,128)(2,1)S(1)}, bf16[640,128]{1,0:T(8,128)(2,1)S(1)}, u32[]{:S(2)}, u32[]{:S(2)}) collective-permute-start(bf16[640,128]{1,0:T(8,128)(2,1)S(1)} %bitcast.96), channel_id=1, source_target_pairs={{0,1},{1,2},{2,3},{3,0},{4,5},{5,6},{6,7},{7,4},{8,9},{9,10},{10,1... | collective-permute-start | bytes 491528 | tf_op jit(solution)/shard_map/ppermute | solution.py:30
  12.6 10.3 %collective-permute-start.1 = (bf16[640,128]{1,0:T(8,128)(2,1)S(1)}, bf16[640,128]{1,0:T(8,128)(2,1)S(1)}, u32[]{:S(2)}, u32[]{:S(2)}) collective-permute-start(bf16[640,128]{1,0:T(8,128)(2,1)S(1)} %bitcast.97), channel_id=1, source_target_pairs={{0,2},{1,3},{2,0},{3,1},{4,6},{5,7},{6,4},{7,5},{8,10},{9,11},{10,... | collective-permute-start | bytes 491528 | tf_op jit(solution)/shard_map/ppermute | solution.py:30
  15.5 7.4 %collective-permute-start = (bf16[640,128]{1,0:T(8,128)(2,1)S(1)}, bf16[640,128]{1,0:T(8,128)(2,1)S(1)}, u32[]{:S(2)}, u32[]{:S(2)}) collective-permute-start(bf16[640,128]{1,0:T(8,128)(2,1)S(1)} %bitcast.98), channel_id=1, source_target_pairs={{0,3},{1,0},{2,1},{3,2},{4,7},{5,4},{6,5},{7,6},{8,11},{9,8},{10,9... | collective-permute-start | bytes 491528 | tf_op jit(solution)/shard_map/ppermute | solution.py:30
  25.9 23.9 %collective-permute-start.4 = (bf16[640,512]{1,0:T(8,128)(2,1)}, bf16[640,512]{1,0:T(8,128)(2,1)S(1)}, u32[]{:S(2)}, u32[]{:S(2)}) collective-permute-start(bf16[640,512]{1,0:T(8,128)(2,1)} %in_order.1.refs_6_), channel_id=1, source_target_pairs={{0,28},{1,29},{2,30},{3,31},{4,0},{5,1},{6,2},{7,3},{8,4},{9,5},{1... | collective-permute-start | bytes 1966088 | tf_op jit(solution)/shard_map/ppermute | solution.py:25
  25.9 23.8 %collective-permute-start.3 = (bf16[640,512]{1,0:T(8,128)(2,1)}, bf16[640,512]{1,0:T(8,128)(2,1)}, u32[]{:S(2)}, u32[]{:S(2)}) collective-permute-start(bf16[640,512]{1,0:T(8,128)(2,1)} %in_order.1.refs_6_), channel_id=1, source_target_pairs={{0,4},{1,5},{2,6},{3,7},{4,8},{5,9},{6,10},{7,11},{8,12},{9,13},{1... | collective-permute-start | bytes 1966088 | tf_op jit(solution)/shard_map/ppermute | solution.py:25
  28.0 1.2 collective-permute-start.5
  29.2 3.5 %collective-permute-start.6 = (f32[2,1]{0,1:T(1,128)S(1)}, f32[2,1]{0,1:T(1,128)S(1)}, u32[]{:S(2)}, u32[]{:S(2)}) collective-permute-start(f32[2,1]{0,1:T(1,128)S(1)} %bitcast_add_fusion), channel_id=1, source_target_pairs={{0,64},{32,96},{64,0},{96,32},{128,192},{160,224},{192,128},{224,1... | collective-permute-start | bytes 32 | tf_op jit(solution)/shard_map/ppermute | solution.py:99
  32.8 5.0 %collective-permute-start.7 = (f32[2,1]{0,1:T(1,128)S(1)}, f32[2,1]{0,1:T(1,128)S(1)}, u32[]{:S(2)}, u32[]{:S(2)}) collective-permute-start(f32[2,1]{0,1:T(1,128)S(1)} %add.232), channel_id=1, source_target_pairs={{0,128},{32,160},{64,192},{96,224},{128,0},{160,32},{192,64},{224,... | collective-permute-start | bytes 32 | tf_op jit(solution)/shard_map/ppermute | solution.py:99
  41.1 17.5 %copy-start.4 = (bf16[256,4096]{1,0:T(8,128)(2,1)S(1)}, bf16[256,4096]{1,0:T(8,128)(2,1)}, u32[]{:S(2)}) copy-start(bf16[256,4096]{1,0:T(8,128)(2,1)} %refs_2_.1) | copy-start | bytes 6291460
  41.1 17.5 %copy-start.10 = (bf16[256,512]{1,0:T(8,128)(2,1)S(1)}, bf16[256,512]{1,0:T(8,128)(2,1)}, u32[]{:S(2)}) copy-start(bf16[256,512]{1,0:T(8,128)(2,1)} %refs_3_.3) | copy-start | bytes 786436
  49.7 8.8 %copy-start.12 = (bf16[640,512]{1,0:T(8,128)(2,1)}, bf16[640,512]{1,0:T(8,128)(2,1)S(1)}, u32[]{:S(2)}) copy-start(bf16[640,512]{1,0:T(8,128)(2,1)S(1)} %collective-permute-done.4.refs_4_) | copy-start | bytes 1966084
  49.7 17.9 %collective-permute-start.8 = (bf16[640,512]{1,0:T(8,128)(2,1)}, bf16[640,512]{1,0:T(8,128)(2,1)}, u32[]{:S(2)}, u32[]{:S(2)}) collective-permute-start(bf16[640,512]{1,0:T(8,128)(2,1)} %collective-permute-done.3.refs_5_), channel_id=1, source_target_pairs={{0,4},{1,5},{2,6},{3,7},{4,8},{5,9},{6,10},{7,11},{8,12},{9,13},{1... | collective-permute-start | bytes 1966088 | tf_op jit(solution)/shard_map/ppermute | solution.py:25
  53.4 16.6 %collective-permute-start.9 = (bf16[640,512]{1,0:T(8,128)(2,1)S(1)}, bf16[640,512]{1,0:T(8,128)(2,1)}, u32[]{:S(2)}, u32[]{:S(2)}) collective-permute-start(bf16[640,512]{1,0:T(8,128)(2,1)S(1)} %collective-permute-done.4.refs_4_), channel_id=1, source_target_pairs={{0,28},{1,29},{2,30},{3,31},{4,0},{5,1},{6,2},{7,3},{8,4},{9,5},{1... | collective-permute-start | bytes 1966088 | tf_op jit(solution)/shard_map/ppermute | solution.py:25
  72.0 84.1 %reduce-scatter.3.cloned.1.call-start = ((), (), s32[]{:S(2)}) async-start(), calls=%async_computation.2 | async-start | bytes 4718592 | tf_op jit(solution)/shard_map/reduce_scatter | solution.py:332
  72.6 21.2 %copy-start.32 = (s32[8]{0:T(128)S(1)}, s32[8]{0:T(128)}, u32[]{:S(2)}) copy-start(s32[8]{0:T(128)} %constant.137.clone) | copy-start | bytes 100
  72.6 21.2 %copy-start.9 = (bf16[640,512]{1,0:T(8,128)(2,1)S(1)}, bf16[640,512]{1,0:T(8,128)(2,1)}, u32[]{:S(2)}) copy-start(bf16[640,512]{1,0:T(8,128)(2,1)} %in_order.1.refs_6_) | copy-start | bytes 1966084
  72.6 85.7 %reduce-scatter.5.cloned.1.call-start = ((), (), s32[]{:S(2)}) async-start(), calls=%async_computation.3 | async-start | bytes 4718592 | tf_op jit(solution)/shard_map/reduce_scatter | solution.py:333
  73.2 15.6 %collective-permute-start.10 = (bf16[640,512]{1,0:T(8,128)(2,1)}, bf16[640,512]{1,0:T(8,128)(2,1)}, u32[]{:S(2)}, u32[]{:S(2)}) collective-permute-start(bf16[640,512]{1,0:T(8,128)(2,1)} %collective-permute-done.8.refs_3_), channel_id=1, source_target_pairs={{0,4},{1,5},{2,6},{3,7},{4,8},{5,9},{6,10},{7,11},{8,12},{9,13},{1... | collective-permute-start | bytes 1966088 | tf_op jit(solution)/shard_map/ppermute | solution.py:25
  76.3 14.7 %collective-permute-start.11 = (bf16[640,512]{1,0:T(8,128)(2,1)}, bf16[640,512]{1,0:T(8,128)(2,1)S(1)}, u32[]{:S(2)}, u32[]{:S(2)}) collective-permute-start(bf16[640,512]{1,0:T(8,128)(2,1)} %collective-permute-done.9.refs_2_), channel_id=1, source_target_pairs={{0,28},{1,29},{2,30},{3,31},{4,0},{5,1},{6,2},{7,3},{8,4},{9,5},{1... | collective-permute-start | bytes 1966088 | tf_op jit(solution)/shard_map/ppermute | solution.py:25
  91.8 14.0 %collective-permute-start.12 = (bf16[640,512]{1,0:T(8,128)(2,1)}, bf16[640,512]{1,0:T(8,128)(2,1)}, u32[]{:S(2)}, u32[]{:S(2)}) collective-permute-start(bf16[640,512]{1,0:T(8,128)(2,1)} %collective-permute-done.10.refs_1_), channel_id=1, source_target_pairs={{0,4},{1,5},{2,6},{3,7},{4,8},{5,9},{6,10},{7,11},{8,12},{9,13},{1... | collective-permute-start | bytes 1966088 | tf_op jit(solution)/shard_map/ppermute | solution.py:25
  110.3 7.3 %collective-permute-start.14 = (bf16[320,512]{1,0:T(8,128)(2,1)S(1)}, bf16[320,512]{1,0:T(8,128)(2,1)S(1)}, u32[]{:S(2)}, u32[]{:S(2)}) collective-permute-start(bf16[320,512]{1,0:T(8,128)(2,1)S(1)} %bitcast.91), channel_id=1, source_target_pairs={{0,28},{1,29},{2,30},{3,31},{4,0},{5,1},{6,2},{7,3},{8,4},{9,5},{1... | collective-permute-start | bytes 983048 | tf_op jit(solution)/shard_map/ppermute | solution.py:25
  110.9 7.1 %collective-permute-start.13 = (bf16[320,512]{1,0:T(8,128)(2,1)S(1)}, bf16[320,512]{1,0:T(8,128)(2,1)S(1)}, u32[]{:S(2)}, u32[]{:S(2)}) collective-permute-start(bf16[320,512]{1,0:T(8,128)(2,1)S(1)} %bitcast.90), channel_id=1, source_target_pairs={{0,4},{1,5},{2,6},{3,7},{4,8},{5,9},{6,10},{7,11},{8,12},{9,13},{1... | collective-permute-start | bytes 983048 | tf_op jit(solution)/shard_map/ppermute | solution.py:25
  120.7 17.8 %collective-permute-start.15 = (bf16[640,512]{1,0:T(8,128)(2,1)}, bf16[640,512]{1,0:T(8,128)(2,1)}, u32[]{:S(2)}, u32[]{:S(2)}) collective-permute-start(bf16[640,512]{1,0:T(8,128)(2,1)} %get-tuple-element.57), channel_id=1, source_target_pairs={{0,4},{1,5},{2,6},{3,7},{4,8},{5,9},{6,10},{7,11},{8,12},{9,13},{1... | collective-permute-start | bytes 1966088 | tf_op jit(solution)/shard_map/ppermute | solution.py:25
  123.8 14.7 %collective-permute-start.16 = (bf16[640,512]{1,0:T(8,128)(2,1)}, bf16[640,512]{1,0:T(8,128)(2,1)}, u32[]{:S(2)}, u32[]{:S(2)}) collective-permute-start(bf16[640,512]{1,0:T(8,128)(2,1)} %get-tuple-element.58), channel_id=1, source_target_pairs={{0,28},{1,29},{2,30},{3,31},{4,0},{5,1},{6,2},{7,3},{8,4},{9,5},{1... | collective-permute-start | bytes 1966088 | tf_op jit(solution)/shard_map/ppermute | solution.py:25
  135.3 8.5 %collective-permute-start.22 = (bf16[192,1024]{1,0:T(8,128)(2,1)S(1)}, bf16[192,1024]{1,0:T(8,128)(2,1)S(1)}, u32[]{:S(2)}, u32[]{:S(2)}) collective-permute-start(bf16[192,1024]{1,0:T(8,128)(2,1)S(1)} %get-tuple-element.96), channel_id=1, source_target_pairs={{0,3},{1,0},{2,1},{3,2},{4,7},{5,4},{6,5},{7,6},{8,11},{9,8},{10,9... | collective-permute-start | bytes 1179656 | tf_op jit(solution)/shard_map/ppermute | solution.py:30
  138.5 9.0 %collective-permute-start.21 = (bf16[192,1024]{1,0:T(8,128)(2,1)S(1)}, bf16[192,1024]{1,0:T(8,128)(2,1)S(1)}, u32[]{:S(2)}, u32[]{:S(2)}) collective-permute-start(bf16[192,1024]{1,0:T(8,128)(2,1)S(1)} %get-tuple-element.97), channel_id=1, source_target_pairs={{0,1},{1,2},{2,3},{3,0},{4,5},{5,6},{6,7},{7,4},{8,9},{9,10},{10,1... | collective-permute-start | bytes 1179656 | tf_op jit(solution)/shard_map/ppermute | solution.py:30
  141.7 12.4 %collective-permute-start.17 = (bf16[640,512]{1,0:T(8,128)(2,1)}, bf16[640,512]{1,0:T(8,128)(2,1)}, u32[]{:S(2)}, u32[]{:S(2)}) collective-permute-start(bf16[640,512]{1,0:T(8,128)(2,1)} %get-tuple-element.59), channel_id=1, source_target_pairs={{0,4},{1,5},{2,6},{3,7},{4,8},{5,9},{6,10},{7,11},{8,12},{9,13},{1... | collective-permute-start | bytes 1966088 | tf_op jit(solution)/shard_map/ppermute | solution.py:25
  143.7 12.4 %collective-permute-start.18 = (bf16[640,512]{1,0:T(8,128)(2,1)}, bf16[640,512]{1,0:T(8,128)(2,1)}, u32[]{:S(2)}, u32[]{:S(2)}) collective-permute-start(bf16[640,512]{1,0:T(8,128)(2,1)} %get-tuple-element.60), channel_id=1, source_target_pairs={{0,28},{1,29},{2,30},{3,31},{4,0},{5,1},{6,2},{7,3},{8,4},{9,5},{1... | collective-permute-start | bytes 1966088 | tf_op jit(solution)/shard_map/ppermute | solution.py:25
  149.0 15.7 %collective-permute-start.23 = (bf16[384,1024]{1,0:T(8,128)(2,1)}, bf16[384,1024]{1,0:T(8,128)(2,1)}, u32[]{:S(2)}, u32[]{:S(2)}) collective-permute-start(bf16[384,1024]{1,0:T(8,128)(2,1)} %get-tuple-element.73), channel_id=1, source_target_pairs={{0,1},{1,2},{2,3},{3,0},{4,5},{5,6},{6,7},{7,4},{8,9},{9,10},{10,1... | collective-permute-start | bytes 2359304 | tf_op jit(solution)/shard_map/ppermute | solution.py:30
  149.0 15.7 %collective-permute-start.24 = (bf16[384,1024]{1,0:T(8,128)(2,1)}, bf16[384,1024]{1,0:T(8,128)(2,1)}, u32[]{:S(2)}, u32[]{:S(2)}) collective-permute-start(bf16[384,1024]{1,0:T(8,128)(2,1)} %get-tuple-element.74), channel_id=1, source_target_pairs={{0,3},{1,0},{2,1},{3,2},{4,7},{5,4},{6,5},{7,6},{8,11},{9,8},{10,9... | collective-permute-start | bytes 2359304 | tf_op jit(solution)/shard_map/ppermute | solution.py:30
  161.6 40.5 %collective-permute-start.19 = (bf16[640,512]{1,0:T(8,128)(2,1)}, bf16[640,512]{1,0:T(8,128)(2,1)}, u32[]{:S(2)}, u32[]{:S(2)}) collective-permute-start(bf16[640,512]{1,0:T(8,128)(2,1)} %get-tuple-element.65), channel_id=1, source_target_pairs={{0,4},{1,5},{2,6},{3,7},{4,8},{5,9},{6,10},{7,11},{8,12},{9,13},{1... | collective-permute-start | bytes 1966088 | tf_op jit(solution)/shard_map/ppermute | solution.py:25
  163.6 39.2 %collective-permute-start.20 = (bf16[640,512]{1,0:T(8,128)(2,1)}, bf16[640,512]{1,0:T(8,128)(2,1)}, u32[]{:S(2)}, u32[]{:S(2)}) collective-permute-start(bf16[640,512]{1,0:T(8,128)(2,1)} %get-tuple-element.66), channel_id=1, source_target_pairs={{0,28},{1,29},{2,30},{3,31},{4,0},{5,1},{6,2},{7,3},{8,4},{9,5},{1... | collective-permute-start | bytes 1966088 | tf_op jit(solution)/shard_map/ppermute | solution.py:25
  167.8 14.4 %collective-permute-start.25 = (bf16[384,128]{1,0:T(8,128)(2,1)S(1)}, bf16[384,128]{1,0:T(8,128)(2,1)S(1)}, u32[]{:S(2)}, u32[]{:S(2)}) collective-permute-start(bf16[384,128]{1,0:T(8,128)(2,1)S(1)} %get-tuple-element.98), channel_id=1, source_target_pairs={{0,16},{1,17},{2,18},{3,19},{4,20},{5,21},{6,22},{7,23},{8,24},{9,... | collective-permute-start | bytes 294920 | tf_op jit(solution)/shard_map/ppermute | solution.py:25
  171.2 17.4 %collective-permute-start.31 = (bf16[384,128]{1,0:T(8,128)(2,1)S(1)}, bf16[384,128]{1,0:T(8,128)(2,1)}, u32[]{:S(2)}, u32[]{:S(2)}) collective-permute-start(bf16[384,128]{1,0:T(8,128)(2,1)S(1)} %get-tuple-element.99), channel_id=1, source_target_pairs={{0,28},{1,29},{2,30},{3,31},{4,0},{5,1},{6,2},{7,3},{8,4},{9,5},{1... | collective-permute-start | bytes 294920 | tf_op jit(solution)/shard_map/ppermute | solution.py:25
  172.2 19.2 %collective-permute-start.30 = (bf16[384,128]{1,0:T(8,128)(2,1)S(1)}, bf16[384,128]{1,0:T(8,128)(2,1)}, u32[]{:S(2)}, u32[]{:S(2)}) collective-permute-start(bf16[384,128]{1,0:T(8,128)(2,1)S(1)} %get-tuple-element.100), channel_id=1, source_target_pairs={{0,4},{1,5},{2,6},{3,7},{4,8},{5,9},{6,10},{7,11},{8,12},{9,13},{1... | collective-permute-start | bytes 294920 | tf_op jit(solution)/shard_map/ppermute | solution.py:25
  182.2 11.8 %collective-permute-start.29 = (bf16[384,128]{1,0:T(8,128)(2,1)S(1)}, bf16[384,128]{1,0:T(8,128)(2,1)}, u32[]{:S(2)}, u32[]{:S(2)}) collective-permute-start(bf16[384,128]{1,0:T(8,128)(2,1)S(1)} %get-tuple-element.101), channel_id=1, source_target_pairs={{0,24},{1,25},{2,26},{3,27},{4,28},{5,29},{6,30},{7,31},{8,0},{9,1... | collective-permute-start | bytes 294920 | tf_op jit(solution)/shard_map/ppermute | solution.py:25
  188.6 7.8 %collective-permute-start.28 = (bf16[384,128]{1,0:T(8,128)(2,1)S(1)}, bf16[384,128]{1,0:T(8,128)(2,1)S(1)}, u32[]{:S(2)}, u32[]{:S(2)}) collective-permute-start(bf16[384,128]{1,0:T(8,128)(2,1)S(1)} %get-tuple-element.102), channel_id=1, source_target_pairs={{0,8},{1,9},{2,10},{3,11},{4,12},{5,13},{6,14},{7,15},{8,16},{9,17... | collective-permute-start | bytes 294920 | tf_op jit(solution)/shard_map/ppermute | solution.py:25
  191.4 8.8 %collective-permute-start.27 = (bf16[384,128]{1,0:T(8,128)(2,1)S(1)}, bf16[384,128]{1,0:T(8,128)(2,1)S(1)}, u32[]{:S(2)}, u32[]{:S(2)}) collective-permute-start(bf16[384,128]{1,0:T(8,128)(2,1)S(1)} %get-tuple-element.103), channel_id=1, source_target_pairs={{0,20},{1,21},{2,22},{3,23},{4,24},{5,25},{6,26},{7,27},{8,28},{9,... | collective-permute-start | bytes 294920 | tf_op jit(solution)/shard_map/ppermute | solution.py:25
  194.0 8.1 %collective-permute-start.26 = (bf16[384,128]{1,0:T(8,128)(2,1)S(1)}, bf16[384,128]{1,0:T(8,128)(2,1)S(1)}, u32[]{:S(2)}, u32[]{:S(2)}) collective-permute-start(bf16[384,128]{1,0:T(8,128)(2,1)S(1)} %get-tuple-element.104), channel_id=1, source_target_pairs={{0,12},{1,13},{2,14},{3,15},{4,16},{5,17},{6,18},{7,19},{8,20},{9,... | collective-permute-start | bytes 294920 | tf_op jit(solution)/shard_map/ppermute | solution.py:25
  204.5 7.6 %copy-start.19 = (bf16[512,512]{0,1:T(8,128)(2,1)S(1)}, bf16[512,512]{0,1:T(8,128)(2,1)}, u32[]{:S(2)}) copy-start(bf16[512,512]{0,1:T(8,128)(2,1)} %reduce-scatter.5.cloned.1.call-done) | copy-start | bytes 1572868
  204.7 8.6 %collective-permute-start.32 = (bf16[640,128]{1,0:T(8,128)(2,1)S(1)}, bf16[640,128]{1,0:T(8,128)(2,1)S(1)}, u32[]{:S(2)}, u32[]{:S(2)}) collective-permute-start(bf16[640,128]{1,0:T(8,128)(2,1)S(1)} %get-tuple-element.105), channel_id=1, source_target_pairs={{0,2},{1,3},{2,0},{3,1},{4,6},{5,7},{6,4},{7,5},{8,10},{9,11},{10,... | collective-permute-start | bytes 491528 | tf_op jit(solution)/shard_map/ppermute | solution.py:30
  207.7 6.5 %collective-permute-start.34 = (bf16[640,128]{1,0:T(8,128)(2,1)S(1)}, bf16[640,128]{1,0:T(8,128)(2,1)S(1)}, u32[]{:S(2)}, u32[]{:S(2)}) collective-permute-start(bf16[640,128]{1,0:T(8,128)(2,1)S(1)} %get-tuple-element.106), channel_id=1, source_target_pairs={{0,3},{1,0},{2,1},{3,2},{4,7},{5,4},{6,5},{7,6},{8,11},{9,8},{10,9... | collective-permute-start | bytes 491528 | tf_op jit(solution)/shard_map/ppermute | solution.py:30
  209.0 6.5 %collective-permute-start.33 = (bf16[640,128]{1,0:T(8,128)(2,1)S(1)}, bf16[640,128]{1,0:T(8,128)(2,1)S(1)}, u32[]{:S(2)}, u32[]{:S(2)}) collective-permute-start(bf16[640,128]{1,0:T(8,128)(2,1)S(1)} %get-tuple-element.107), channel_id=1, source_target_pairs={{0,1},{1,2},{2,3},{3,0},{4,5},{5,6},{6,7},{7,4},{8,9},{9,10},{10,1... | collective-permute-start | bytes 491528 | tf_op jit(solution)/shard_map/ppermute | solution.py:30
  (24 other events, 78.7 us)
Sparse Core Ops, SparseCore 0:
  11.0 41.6 all-gather.2
  72.2 42.4 all-gather.4
Sparse Core Ops, SparseCore 1:
  75.0 41.5 reduce-scatter.2
  119.0 39.3 reduce-scatter.4
